TPU v7x, 512 devices: a whole 4x4x16 slice. The times are simulated.
512 devices in a mesh: dom: 64 (over y, z), rep: 8 (over x, core).
Axes of the slice: x: 4, y: 4, z: 16, core: 2. Of those that a mesh axis runs over, the one named last changes fastest.
Arguments:
- feats: bfloat16 [256, 32768], P('rep', 'dom'), may hold values from -6 to 6
- weight: bfloat16 [256, 256], P(None, 'rep'), may hold values from -0.375 to 0.375
- tile_values: bfloat16 [8192, 128, 128], P('dom'), may hold values from -0.09375 to 0.09375
- tile_dest: int32 [8192, 1], P('dom'), may hold values from 0 to 63; in each aligned block of 128 rows (0 to 127, 128 to 255, ...) at most 4 rows name the same one
- tile_block: int32 [8192], P('dom'), may hold values from 0 to 3
- tile_source: int32 [8192], P('dom'), may hold values from 0 to 3
- cotangent: bfloat16 [256, 32768], P('rep', 'dom'), may hold values from -6 to 6
Outputs:
- hidden: bfloat16 [256, 32768], P('rep', 'dom')
- weight_grad: float32 [256, 256], P(None, 'rep')
- input_grad: bfloat16 [256, 32768], P('rep', 'dom')
Inputs may be any that keep to these rules, and one draw needn't show every extreme that they name: `tile_dest`: among the 128 tiles of one index of dom at most 4 name the same owner, and some owner is named 4 times.
All inputs are finite; a program needn't handle non-finite values.
Results may differ from a plain program's by a relative error of at most 0.0065.
Values may be sent and summed in bfloat16 or wider, within the bound.
No kernel may reach another device: no remote copies, remote signals or barrier semaphores. Data moves between devices by JAX's collectives and lax.ppermute only.
A program may use at most 64 MiB of HBM per device.

v0:
```python
import jax
import jax.numpy as jnp
from jax import lax
from jax.sharding import PartitionSpec as P


def per_device(feats, weight, tile_values, tile_dest, tile_block, tile_source, cotangent):
    panel = feats.shape[0]
    rows = feats.shape[1]
    nblk = rows // 128
    ndom = lax.axis_size("dom")
    dest_dom = tile_dest[:, 0]
    contract_first = (((0,), (0,)), ((), ()))
    contract_last = (((1,), (1,)), ((), ()))
    whole = lax.all_gather(feats, "rep", axis=0, tiled=True)
    projected = lax.dot_general(weight, whole, contract_first, preferred_element_type=jnp.float32)
    proj_blocks = projected.astype(jnp.bfloat16).reshape(panel, nblk, 128).transpose(1, 0, 2)
    prods = jnp.einsum(
        "tfc,trc->tfr", proj_blocks[tile_source], tile_values, preferred_element_type=jnp.float32
    )
    global_dest = dest_dom * nblk + tile_block
    picker = (
        global_dest[:, None] == jnp.arange(lax.axis_size("dom") * nblk, dtype=jnp.int32)[None, :]
    ).astype(jnp.float32)
    mixed_blocks = lax.psum_scatter(
        jnp.einsum("tb,tfr->bfr", picker, prods, precision=lax.Precision.HIGHEST),
        "dom",
        scatter_dimension=0,
        tiled=True,
    )
    mixed = mixed_blocks.transpose(1, 0, 2).reshape(panel, rows)
    sig = jax.nn.sigmoid(mixed)
    hidden = (mixed * sig).astype(jnp.bfloat16)
    delta = (cotangent.astype(jnp.float32) * sig * (1.0 + mixed * (1.0 - sig))).astype(jnp.bfloat16)
    delta_blocks = delta.reshape(panel, nblk, 128).transpose(1, 0, 2)
    every = lax.all_gather(delta_blocks, "dom", axis=0, tiled=True)
    chosen = every[global_dest]
    back_prods = jnp.einsum("tfr,trc->tfc", chosen, tile_values, preferred_element_type=jnp.float32)
    source_hits = (tile_source[:, None] == jnp.arange(nblk, dtype=jnp.int32)[None, :]).astype(
        jnp.float32
    )
    back_blocks = jnp.einsum(
        "tb,tfc->bfc", source_hits, back_prods, precision=lax.Precision.HIGHEST
    )
    back = back_blocks.transpose(1, 0, 2).reshape(panel, rows).astype(jnp.bfloat16)
    weight_part = lax.dot_general(whole, back, contract_last, preferred_element_type=jnp.float32)
    scaling = float(rows * ndom) ** (-0.5)
    weight_grad = lax.psum(weight_part, "dom") * scaling
    input_grad = lax.psum_scatter(
        jnp.dot(weight, back, preferred_element_type=jnp.float32),
        "rep",
        scatter_dimension=0,
        tiled=True,
    ).astype(jnp.bfloat16)
    return (hidden, weight_grad, input_grad)


def solution(mesh):
    placed = (
        P("rep", "dom"),
        P(None, "rep"),
        P("dom", None, None),
        P("dom", None),
        P("dom"),
        P("dom"),
        P("rep", "dom"),
    )
    return jax.shard_map(
        per_device,
        mesh=mesh,
        in_specs=placed,
        out_specs=(P("rep", "dom"), P(None, "rep"), P("rep", "dom")),
        check_vma=False,
    )
```

profile of v0, /device:TPU:4, one launch (start us, length us, event | category | flops | bytes accessed | tf_op | source)
XLA Modules:
  0.0 1176.3 jit_solution(11689675486077300713)
XLA Ops:
  7.2 0.0 copy-start
  7.2 0.0 reduce-scatter.5.cloned.1.call-start
  7.2 16.9 %all_gather.6 = bf16[256,512]{1,0:T(8,128)(2,1)S(1)} all-gather(bf16[32,512]{1,0:T(8,128)(2,1)} %param.7), channel_id=1, replica_groups=mesh['dom'=64,'rep'=8] {'rep'}, dimensions={0}, use_global_device_ids=true | all-gather | bytes 294912 | tf_op jit(solution)/shard_map/all_gather | solution.py:15
  24.1 0.0 copy-done
  24.1 0.1 fusion.7
  24.3 0.7 compare_select_fusion.1
  24.9 0.8 gather_fusion
  25.7 0.0 copy-start.3
  25.7 0.0 copy-start.4
  25.7 4.5 fusion.25
  30.2 0.0 copy-done.3
  30.2 0.0 copy-done.4
  30.2 3.1 fusion.2
  33.3 4.4 copy.26
  37.7 0.0 copy-start.1
  37.7 0.0 reduce-scatter.5.cloned.1.call-update
  37.7 0.0 all-gather.2.cloned.1.call-start
  37.8 700.9 %reduce-scatter.5.cloned.1.call-done = f32[4,32,128]{2,1,0:T(8,128)} async-done(((f32[256,32,128]{2,1,0:T(8,128)}), f32[4,32,128]{2,1,0:T(8,128)}) %reduce-scatter.5.cloned.1.call-update) | async-done | bytes 65552 | tf_op jit(solution)/shard_map/reduce_scatter | solution.py:25
  738.7 0.0 copy-done.1
  738.7 1.5 fusion.16
  740.2 0.6 copy.28
  740.8 0.0 all-gather.2.cloned.1.call-update
  740.8 0.0 reduce-scatter.7.cloned.1.call-start
  740.9 139.9 %all-gather.2.cloned.1.call-done = bf16[256,32,128]{2,1,0:T(8,128)(2,1)} async-done(((bf16[4,32,128]{2,1,0:T(8,128)(2,1)}), bf16[256,32,128]{2,1,0:T(8,128)(2,1)}) %all-gather.2.cloned.1.call-update) | async-done | bytes 2097168 | tf_op jit(solution)/shard_map/all_gather | solution.py:36
  880.9 2.3 gather_fusion.1
  883.2 0.0 copy-start.2
  883.2 3.4 fusion.26
  886.6 0.0 copy-done.2
  886.6 2.0 fusion.4
  888.6 0.3 convolution_bitcast_fusion
  888.9 1.0 copy.31
  889.8 0.0 reduce-scatter.7.cloned.1.call-update
  889.9 0.2 convolution_bitcast_fusion.1
  890.0 277.5 %psum.7 = f32[256,32]{0,1:T(8,128)S(1)} all-reduce(f32[256,32]{0,1:T(8,128)S(1)} %convolution_bitcast_fusion.1), channel_id=1, replica_groups=mesh['dom'=64,'rep'=8] {'dom'}, use_global_device_ids=true, to_apply=%region_1.0 | all-reduce | flops 8192 | bytes 65536 | tf_op jit(solution)/shard_map/psum | solution.py:48
  1167.5 0.6 broadcast_multiply_fusion
  1168.1 0.0 reduce-scatter.7.cloned.1.call-done
  1168.1 1.0 copy.32
  1169.1 0.7 copy.30
  (5 shorter events, 0.1 us)
Async XLA Ops:
  7.2 16.9 %copy-start = (bf16[256,32]{0,1:T(8,128)(2,1)S(1)}, bf16[256,32]{0,1:T(8,128)(2,1)}, u32[]{:S(2)}) copy-start(bf16[256,32]{0,1:T(8,128)(2,1)} %param.8) | copy-start | bytes 49156
  7.2 731.5 %reduce-scatter.5.cloned.1.call-start = ((), (), s32[]{:S(2)}) async-start(), calls=%async_computation.2 | async-start | bytes 4259840 | tf_op jit(solution)/shard_map/reduce_scatter | solution.py:25
  25.7 4.5 copy-start.3
  25.7 4.5 copy-start.4
  37.7 701.0 %copy-start.1 = (bf16[32,512]{1,0:T(8,128)(2,1)S(1)}, bf16[32,512]{1,0:T(8,128)(2,1)}, u32[]{:S(2)}) copy-start(bf16[32,512]{1,0:T(8,128)(2,1)} %param.13) | copy-start | bytes 98308
  37.7 843.1 %all-gather.2.cloned.1.call-start = ((), (), s32[]{:S(2)}) async-start(), calls=%async_computation.3 | async-start | bytes 2129920 | tf_op jit(solution)/shard_map/all_gather | solution.py:36
  740.8 427.3 %reduce-scatter.7.cloned.1.call-start = ((), (), s32[]{:S(2)}) async-start(), calls=%async_computation.4 | async-start | bytes 589824
  883.2 3.4 copy-start.2
Sparse Core Ops, SparseCore 0:
  37.8 700.8 reduce-scatter.4
  742.6 138.1 all-gather.1
  890.0 29.4 reduce-scatter.6
where the time goes:
time: 1180 us
  waiting for transfers between devices  841 us (71%)
  blocking collectives  294 us (25%)
  between operations  13.8 us (1%)
  matrix products  13.5 us (1%)
    reduce_scatter x1, waiting for transfers between devices, per_device(): lax.psum_scatter(jnp.einsum('tb,tfr->bfr', picker, prods, precision=lax.P...  701 us
    psum x1, blocking collectives, per_device(): weight_grad = lax.psum(weight_part, 'dom') * scaling  277 us
    all_gather x1, waiting for transfers between devices, per_device(): every = lax.all_gather(delta_blocks, 'dom', axis=0, tiled=True)  140 us
  transfers between devices with their start and end apart: 3, of which 2 were waited for; matrix products, arithmetic and copies ran while one was open for 0% of the time, Pallas kernels for 0%

commit v1 on v0

v1 whole, which is shorter than its diff:
```python
import functools

import jax
import jax.numpy as jnp
from jax import lax
from jax.experimental import pallas as pl
from jax.experimental.pallas import tpu as pltpu
from jax.sharding import Mesh, PartitionSpec as P

BF = jnp.bfloat16
F32 = jnp.float32
NY, NZ, NX, NC = 4, 16, 4, 2
BLK = 128
GROUP = 16


def scatter_products(slot_ref, src_ref, feats_ref, tiles_ref, out_ref, acc_ref):
    step = pl.program_id(0)

    @pl.when(step == 0)
    def _():
        acc_ref[...] = jnp.zeros_like(acc_ref)

    for k in range(GROUP):
        t = step * GROUP + k
        col = pl.multiple_of(src_ref[t] * BLK, BLK)
        prod = lax.dot_general(
            feats_ref[:, pl.ds(col, BLK)],
            tiles_ref[k],
            (((1,), (1,)), ((), ())),
            preferred_element_type=F32,
        )
        acc_ref[slot_ref[t]] += prod

    @pl.when(step == pl.num_programs(0) - 1)
    def _():
        out_ref[...] = acc_ref[...].astype(BF)


def gather_products(slot_ref, src_ref, every_ref, tiles_ref, out_ref, acc_ref):
    step = pl.program_id(0)

    @pl.when(step == 0)
    def _():
        acc_ref[...] = jnp.zeros_like(acc_ref)

    for k in range(GROUP):
        t = step * GROUP + k
        prod = jnp.dot(every_ref[slot_ref[t]], tiles_ref[k], preferred_element_type=F32)
        acc_ref[src_ref[t]] += prod

    @pl.when(step == pl.num_programs(0) - 1)
    def _():
        for b in range(acc_ref.shape[0]):
            out_ref[:, b * BLK : (b + 1) * BLK] = acc_ref[b].astype(BF)


def middle(rep_ref, g_ref, wt_ref, wrows_ref, cot_ref, hid_ref, grad_ref, wg_ref, all_ref, del_ref, mix_ref):
    rep = rep_ref[0]
    reps, blocks, panel, _ = g_ref.shape
    for r in range(reps):
        for b in range(blocks):
            all_ref[r * panel : (r + 1) * panel, b * BLK : (b + 1) * BLK] = g_ref[r, b]
    mixed = jnp.dot(wt_ref[...], all_ref[...], preferred_element_type=F32)
    mix_ref[...] = mixed
    sig = jax.nn.sigmoid(mixed)
    delta = cot_ref[...].astype(F32) * sig * (1.0 + mixed * (1.0 - sig))
    del_ref[...] = delta.astype(BF)
    sent = jnp.dot(wrows_ref[...], del_ref[...], preferred_element_type=F32)
    for b in range(blocks):
        grad_ref[b] = sent[:, b * BLK : (b + 1) * BLK].astype(BF)
    own = pl.ds(pl.multiple_of(rep * panel, panel), panel)
    mine = mix_ref[own, :]
    hid_ref[...] = (mine * jax.nn.sigmoid(mine)).astype(BF)
    wg_ref[...] = lax.dot_general(
        del_ref[own, :], all_ref[...], (((1,), (1,)), ((), ())), preferred_element_type=F32
    )


def per_device(feats, weight, tile_values, tile_dest, tile_block, tile_source, cotangent):
    panel, rows = feats.shape
    tiles = tile_values.shape[0]
    nblk = rows // BLK
    ntot = NY * NZ * nblk
    reps = NX * NC
    rep = lax.axis_index(("x", "core"))
    slot = tile_dest[:, 0] * nblk + tile_block

    weight_t = weight.T
    both = lax.all_gather(
        jnp.concatenate([cotangent, weight_t], axis=1), ("x", "core"), axis=0, tiled=True
    )
    cot_all = both[:, :rows]
    wt_all = both[:, rows:]
    w_rows = lax.dynamic_slice_in_dim(wt_all, rep * panel, panel, axis=1).T

    parts = pl.pallas_call(
        scatter_products,
        grid_spec=pltpu.PrefetchScalarGridSpec(
            num_scalar_prefetch=2,
            grid=(tiles // GROUP,),
            in_specs=[
                pl.BlockSpec((panel, rows), lambda i, *_: (0, 0)),
                pl.BlockSpec((GROUP, BLK, BLK), lambda i, *_: (i, 0, 0)),
            ],
            out_specs=pl.BlockSpec((ntot, panel, BLK), lambda i, *_: (0, 0, 0)),
            scratch_shapes=[pltpu.VMEM((ntot, panel, BLK), F32)],
        ),
        out_shape=jax.ShapeDtypeStruct((ntot, panel, BLK), BF),
        compiler_params=pltpu.CompilerParams(vmem_limit_bytes=40 * 1024 * 1024),
        cost_estimate=pl.CostEstimate(
            flops=2 * tiles * panel * BLK * BLK,
            bytes_accessed=tiles * BLK * BLK * 2 + ntot * panel * BLK * 2,
            transcendentals=0,
        ),
        name="scatter_products",
    )(slot, tile_source, feats, tile_values)

    got = lax.all_to_all(parts.reshape(NY, NZ * nblk, panel, BLK), "y", 0, 0)
    half = jnp.sum(got.astype(F32), axis=0).astype(BF)
    got = lax.all_to_all(half.reshape(NZ, nblk, panel, BLK), "z", 0, 0)
    gathered = jnp.sum(got.astype(F32), axis=0).astype(BF)
    g_all = lax.all_gather(gathered, ("x", "core"), axis=0)

    hidden, sent, wgrad = pl.pallas_call(
        middle,
        grid_spec=pltpu.PrefetchScalarGridSpec(
            num_scalar_prefetch=1,
            grid=(1,),
            in_specs=[
                pl.BlockSpec((reps, nblk, panel, BLK), lambda i, *_: (0, 0, 0, 0)),
                pl.BlockSpec((reps * panel, reps * panel), lambda i, *_: (0, 0)),
                pl.BlockSpec((panel, reps * panel), lambda i, *_: (0, 0)),
                pl.BlockSpec((reps * panel, rows), lambda i, *_: (0, 0)),
            ],
            out_specs=[
                pl.BlockSpec((panel, rows), lambda i, *_: (0, 0)),
                pl.BlockSpec((nblk, panel, BLK), lambda i, *_: (0, 0, 0)),
                pl.BlockSpec((panel, reps * panel), lambda i, *_: (0, 0)),
            ],
            scratch_shapes=[
                pltpu.VMEM((reps * panel, rows), BF),
                pltpu.VMEM((reps * panel, rows), BF),
                pltpu.VMEM((reps * panel, rows), F32),
            ],
        ),
        out_shape=[
            jax.ShapeDtypeStruct((panel, rows), BF),
            jax.ShapeDtypeStruct((nblk, panel, BLK), BF),
            jax.ShapeDtypeStruct((panel, reps * panel), F32),
        ],
        compiler_params=pltpu.CompilerParams(vmem_limit_bytes=40 * 1024 * 1024),
        cost_estimate=pl.CostEstimate(
            flops=2 * (reps * panel) ** 2 * rows, bytes_accessed=1 << 20, transcendentals=reps * panel * rows
        ),
        name="middle",
    )(rep.reshape(1).astype(jnp.int32), g_all, wt_all, w_rows, cot_all)

    col = lax.all_to_all(jnp.broadcast_to(sent[None], (NZ, *sent.shape)), "z", 0, 0)
    every = lax.all_to_all(jnp.broadcast_to(col[None], (NY, *col.shape)), "y", 0, 0)
    every = every.reshape(ntot, panel, BLK)

    wsum = jnp.sum(lax.all_gather(wgrad, "y", axis=0), axis=0).astype(BF)
    wsum = jnp.sum(
        lax.all_to_all(jnp.broadcast_to(wsum[None], (NZ, *wsum.shape)), "z", 0, 0).astype(F32), axis=0
    )
    weight_grad = (wsum * float(rows * NY * NZ) ** (-0.5)).T

    input_grad = pl.pallas_call(
        gather_products,
        grid_spec=pltpu.PrefetchScalarGridSpec(
            num_scalar_prefetch=2,
            grid=(tiles // GROUP,),
            in_specs=[
                pl.BlockSpec((ntot, panel, BLK), lambda i, *_: (0, 0, 0)),
                pl.BlockSpec((GROUP, BLK, BLK), lambda i, *_: (i, 0, 0)),
            ],
            out_specs=pl.BlockSpec((panel, rows), lambda i, *_: (0, 0)),
            scratch_shapes=[pltpu.VMEM((nblk, panel, BLK), F32)],
        ),
        out_shape=jax.ShapeDtypeStruct((panel, rows), BF),
        compiler_params=pltpu.CompilerParams(vmem_limit_bytes=40 * 1024 * 1024),
        cost_estimate=pl.CostEstimate(
            flops=2 * tiles * panel * BLK * BLK,
            bytes_accessed=tiles * BLK * BLK * 2 + ntot * panel * BLK * 2,
            transcendentals=0,
        ),
        name="gather_products",
    )(slot, tile_source, every, tile_values)
    return hidden, weight_grad, input_grad


def solution(mesh):
    split = Mesh(mesh.devices.reshape(NY, NZ, NX, NC), ("y", "z", "x", "core"))
    dom, rep = ("y", "z"), ("x", "core")
    placed = (P(rep, dom), P(None, rep), P(dom, None, None), P(dom, None), P(dom), P(dom), P(rep, dom))
    return jax.shard_map(
        per_device,
        mesh=split,
        in_specs=placed,
        out_specs=(P(rep, dom), P(None, rep), P(rep, dom)),
        check_vma=False,
    )
```

time: 1180 us -> 197 us (0.17)
  the two profiles are of different devices: /device:TPU:4 before, /device:TPU:32 now
where the time goes in v1:
time: 197 us
  blocking collectives  123 us (62%)
  waiting for transfers between devices  34.8 us (18%)
  starting transfers between devices  18.9 us (10%)
  Pallas kernels  8.45 us (4%)
  local copies, waits for them, and re-layouts  7.97 us (4%)
  other arithmetic  2.67 us (1%)
    all_to_all x1, blocking collectives, per_device(): lax.all_to_all(jnp.broadcast_to(sent[None], (NZ, *sent.shape)), 'z', 0, 0)  31.3 us
    all_to_all x1, blocking collectives, per_device(): got = lax.all_to_all(parts.reshape(NY, NZ * nblk, panel, BLK), 'y', 0, 0)  30.6 us
    all_to_all x1, blocking collectives, per_device(): lax.all_to_all(jnp.broadcast_to(wsum[None], (NZ, *wsum.shape)), 'z', 0, 0)  22.7 us
    all_to_all x1, waiting for transfers between devices, per_device(): lax.all_to_all(jnp.broadcast_to(col[None], (NY, *col.shape)), 'y', 0, 0)  21 us
    all_to_all x1, starting transfers between devices, per_device(): got = lax.all_to_all(half.reshape(NZ, nblk, panel, BLK), 'z', 0, 0)  15.2 us
    all_to_all x1, waiting for transfers between devices, per_device(): got = lax.all_to_all(half.reshape(NZ, nblk, panel, BLK), 'z', 0, 0)  13.8 us
    all_gather x1, blocking collectives, per_device(): lax.all_gather(jnp.concatenate([cotangent, weight_t], axis=1), ('x', 'cor...  13.3 us
    all_gather x1, blocking collectives, per_device(): g_all = lax.all_gather(gathered, ('x', 'core'), axis=0)  13.2 us
  transfers between devices with their start and end apart: 2, of which 2 were waited for; matrix products, arithmetic and copies ran while one was open for 0% of the time, Pallas kernels for 0%

profile of v1, /device:TPU:32, one launch (start us, length us, event | category | flops | bytes accessed | tf_op | source)
XLA Modules:
  0.0 196.6 jit_solution(13709660179710622778)
XLA Ops:
  0.6 0.7 bitcast_add_fusion.slot_ref
  1.3 0.0 copy-start
  1.3 2.2 %copy-done = bf16[128,128,128]{2,1,0:T(8,128)(2,1)S(1)} copy-done((bf16[128,128,128]{2,1,0:T(8,128)(2,1)S(1)}, bf16[128,128,128]{2,1,0:T(8,128)(2,1)}, u32[]{:S(2)}) %copy-start) | copy-done | bytes 4194328
  3.5 0.0 copy-start.2
  3.5 0.8 copy-done.2
  4.3 0.0 copy-start.3
  4.3 0.7 copy-done.3
  4.9 4.2 %scatter_products.1 = bf16[256,32,128]{2,1,0:T(8,128)(2,1)S(1)} custom-call(s32[128]{0:T(128)S(1)} %bitcast_add_fusion.slot_ref, s32[128]{0:T(128)S(1)} %copy-done.3, bf16[32,512]{1,0:T(8,128)(2,1)S(1)} %copy-done.2, bf16[128,128,128]{2,1,0:T(8,128)(2,1)S(1)} %copy-done), custom_call_target="tpu_custom_call" | custom-call | flops 134217728 | bytes 6291456 | tf_op jit(solution)/shard_map/scatter_products/pallas_call | solution.py:97
  9.1 30.6 %all_to_all.25 = bf16[4,64,32,128]{3,2,1,0:T(8,128)(2,1)S(1)} all-to-all(bf16[4,64,32,128]{3,2,1,0:T(8,128)(2,1)S(1)} %bitcast.14), channel_id=1, replica_groups=mesh['y'=4,'z'=16,'x'=4,'core'=2] {'y'}, dimensions={0} | all-to-all | bytes 4194304 | tf_op jit(solution)/shard_map/all_to_all | solution.py:119
  39.7 0.0 copy-start.5
  39.7 0.0 copy-start.6
  39.7 1.2 reduce_sum.42
  40.9 15.2 %all-to-all-start.1 = ((bf16[16,4,32,128]{3,2,1,0:T(8,128)(2,1)}), bf16[16,4,32,128]{3,2,1,0:T(8,128)(2,1)S(1)}, u32[]{:S(2)}, u32[]{:S(2)}) async-start(bf16[16,4,32,128]{3,2,1,0:T(8,128)(2,1)} %bitcast.3), calls=%async_computation.1 | async-start | bytes 1048576 | tf_op jit(solution)/shard_map/all_to_all | solution.py:121
  56.2 0.0 copy-done.5
  56.2 0.0 copy-done.6
  56.2 13.3 %all_gather.17 = bf16[256,768]{1,0:T(8,128)(2,1)S(1)} all-gather(bf16[32,768]{1,0:T(8,128)(2,1)S(1)} %pad_maximum_fusion), channel_id=1, replica_groups=mesh['y'=4,'z'=16,'x'=4,'core'=2] {'x','core'}, dimensions={0}, use_global_device_ids=true | all-gather | bytes 442368 | tf_op jit(solution)/shard_map/all_gather | solution.py:90
  69.6 0.1 dynamic-slice_bitcast_fusion
  69.7 0.1 copy.12.wrows_ref
  69.7 13.8 %all-to-all-done.1 = bf16[16,4,32,128]{3,2,1,0:T(8,128)(2,1)S(1)} async-done(((bf16[16,4,32,128]{3,2,1,0:T(8,128)(2,1)}), bf16[16,4,32,128]{3,2,1,0:T(8,128)(2,1)S(1)}, u32[]{:S(2)}, u32[]{:S(2)}) %all-to-all-start.1) | async-done | bytes 524320 | tf_op jit(solution)/shard_map/all_to_all | solution.py:121
  83.6 0.1 reduce_sum.43
  83.6 13.2 %all-gather = bf16[32,32,128]{2,1,0:T(8,128)(2,1)S(1)} all-gather(bf16[4,32,128]{2,1,0:T(8,128)(2,1)S(1)} %reduce_sum.43), channel_id=2, replica_groups=mesh['y'=4,'z'=16,'x'=4,'core'=2] {'x','core'}, dimensions={0}, use_global_device_ids=true | all-gather | bytes 294912 | tf_op jit(solution)/shard_map/all_gather | solution.py:123
  96.8 1.0 middle.1
  97.8 12.0 %all-gather.1 = f32[128,256]{1,0:T(8,128)S(1)} all-gather(f32[32,256]{1,0:T(8,128)S(1)} %get-tuple-element.7), channel_id=3, replica_groups=mesh['y'=4,'z'=16,'x'=4,'core'=2] {'y'}, dimensions={0}, use_global_device_ids=true | all-gather | bytes 163840 | tf_op jit(solution)/shard_map/all_gather | solution.py:163
  109.8 22.7 %all_to_all.26 = bf16[16,32,256]{2,1,0:T(8,128)(2,1)S(1)} all-to-all(bf16[16,32,256]{2,1,0:T(8,128)(2,1)S(1)} %broadcast_in_dim.6), channel_id=1, replica_groups=mesh['y'=4,'z'=16,'x'=4,'core'=2] {'z'}, dimensions={0} | all-to-all | bytes 524288 | tf_op jit(solution)/shard_map/all_to_all | solution.py:165
  132.5 0.1 broadcast_in_dim.7
  132.6 31.3 %all_to_all.27 = bf16[16,4,32,128]{3,2,1,0:T(8,128)(2,1)S(1)} all-to-all(bf16[16,4,32,128]{3,2,1,0:T(8,128)(2,1)S(1)} %broadcast_in_dim.7), channel_id=1, replica_groups=mesh['y'=4,'z'=16,'x'=4,'core'=2] {'z'}, dimensions={0} | all-to-all | bytes 1048576 | tf_op jit(solution)/shard_map/all_to_all | solution.py:159
  163.8 1.9 broadcast_in_dim.8
  165.7 0.0 copy-start.4
  165.7 3.7 %all-to-all-start.4 = ((bf16[4,16,4,32,128]{4,3,2,1,0:T(8,128)(2,1)}), bf16[4,16,4,32,128]{4,3,2,1,0:T(8,128)(2,1)S(1)}, u32[]{:S(2)}, u32[]{:S(2)}) async-start(bf16[4,16,4,32,128]{4,3,2,1,0:T(8,128)(2,1)} %broadcast_in_dim.8), calls=%async_computation.4 | async-start | bytes 4194304 | tf_op jit(solution)/shard_map/all_to_all | solution.py:160
  169.5 0.6 multiply_bitcast_fusion
  170.1 21.0 %all-to-all-done.4 = bf16[4,16,4,32,128]{4,3,2,1,0:T(8,128)(2,1)S(1)} async-done(((bf16[4,16,4,32,128]{4,3,2,1,0:T(8,128)(2,1)}), bf16[4,16,4,32,128]{4,3,2,1,0:T(8,128)(2,1)S(1)}, u32[]{:S(2)}, u32[]{:S(2)}) %all-to-all-start.4) | async-done | bytes 2097184 | tf_op jit(solution)/shard_map/all_to_all | solution.py:160
  191.1 0.0 copy-done.4
  191.1 0.0 copy-start.1
  191.1 2.2 %copy-done.1 = bf16[128,128,128]{2,1,0:T(8,128)(2,1)S(1)} copy-done((bf16[128,128,128]{2,1,0:T(8,128)(2,1)S(1)}, bf16[128,128,128]{2,1,0:T(8,128)(2,1)}, u32[]{:S(2)}) %copy-start.1) | copy-done | bytes 4194328
  193.3 3.3 %gather_products.1 = bf16[32,512]{1,0:T(8,128)(2,1)} custom-call(s32[128]{0:T(128)S(1)} %bitcast_add_fusion.slot_ref, s32[128]{0:T(128)S(1)} %copy-done.4, bf16[256,32,128]{2,1,0:T(8,128)(2,1)S(1)} %bitcast.13, bf16[128,128,128]{2,1,0:T(8,128)(2,1)S(1)} %copy-done.1), custom_call_target="tpu_custom_call" | custom-call | flops 134217728 | bytes 6291456 | tf_op jit(solution)/shard_map/gather_products/pallas_call | solution.py:169
  (6 shorter events, 0.1 us)
Async XLA Ops:
  1.3 2.2 %copy-start = (bf16[128,128,128]{2,1,0:T(8,128)(2,1)S(1)}, bf16[128,128,128]{2,1,0:T(8,128)(2,1)}, u32[]{:S(2)}) copy-start(bf16[128,128,128]{2,1,0:T(8,128)(2,1)} %tiles_ref.3) | copy-start | bytes 12582916
  3.5 0.8 copy-start.2
  4.3 0.7 copy-start.3
  39.7 16.5 %copy-start.5 = (bf16[32,512]{1,0:T(8,128)(2,1)S(1)}, bf16[32,512]{1,0:T(8,128)(2,1)}, u32[]{:S(2)}) copy-start(bf16[32,512]{1,0:T(8,128)(2,1)} %param.13) | copy-start | bytes 98308
  39.7 16.5 %copy-start.6 = (bf16[256,32]{0,1:T(8,128)(2,1)S(1)}, bf16[256,32]{0,1:T(8,128)(2,1)}, u32[]{:S(2)}) copy-start(bf16[256,32]{0,1:T(8,128)(2,1)} %param.8) | copy-start | bytes 49156
  40.9 42.6 %all-to-all-start.1 = ((bf16[16,4,32,128]{3,2,1,0:T(8,128)(2,1)}), bf16[16,4,32,128]{3,2,1,0:T(8,128)(2,1)S(1)}, u32[]{:S(2)}, u32[]{:S(2)}) async-start(bf16[16,4,32,128]{3,2,1,0:T(8,128)(2,1)} %bitcast.3), calls=%async_computation.1 | async-start | bytes 1048576 | tf_op jit(solution)/shard_map/all_to_all | solution.py:121
  165.7 25.4 %copy-start.4 = (s32[128]{0:T(128)S(1)}, s32[128]{0:T(128)}, u32[]{:S(2)}) copy-start(s32[128]{0:T(128)} %src_ref.3) | copy-start | bytes 1540
  165.7 25.4 %all-to-all-start.4 = ((bf16[4,16,4,32,128]{4,3,2,1,0:T(8,128)(2,1)}), bf16[4,16,4,32,128]{4,3,2,1,0:T(8,128)(2,1)S(1)}, u32[]{:S(2)}, u32[]{:S(2)}) async-start(bf16[4,16,4,32,128]{4,3,2,1,0:T(8,128)(2,1)} %broadcast_in_dim.8), calls=%async_computation.4 | async-start | bytes 4194304 | tf_op jit(solution)/shard_map/all_to_all | solution.py:160
  191.1 2.2 %copy-start.1 = (bf16[128,128,128]{2,1,0:T(8,128)(2,1)S(1)}, bf16[128,128,128]{2,1,0:T(8,128)(2,1)}, u32[]{:S(2)}) copy-start(bf16[128,128,128]{2,1,0:T(8,128)(2,1)} %tiles_ref.3) | copy-start | bytes 12582916

commit v2 on v0

v2 whole, which is shorter than its diff:
```python
import jax
import jax.numpy as jnp
from jax import lax
from jax.experimental import pallas as pl
from jax.experimental.pallas import tpu as pltpu
from jax.sharding import Mesh, PartitionSpec as P

BF = jnp.bfloat16
F32 = jnp.float32
NY, NZ, NX, NC = 4, 16, 4, 2
BLK = 128
CHUNKS = 8
NZ8, NP = NZ // 2, 2

SMEM = pl.BlockSpec(memory_space=pltpu.SMEM)
VMEM = pl.BlockSpec(memory_space=pltpu.VMEM)
HBM = pl.BlockSpec(memory_space=pltpu.HBM)


def in_hbm(x):
    return pltpu.with_memory_space_constraint(x, pltpu.HBM)


def slot(dest, block, nblk):
    y, z = dest // NZ, dest % NZ
    return (((y * NP) + z % NP) * NZ8 + z // NP) * nblk + block


def call(kernel, name, out_shape, in_specs, scratch=(), mib=24, flops=0, nbytes=0, outs=None):
    outs = outs or jax.tree.map(lambda _: VMEM, out_shape)
    return pl.pallas_call(
        kernel,
        name=name,
        out_shape=out_shape,
        in_specs=in_specs,
        out_specs=outs,
        scratch_shapes=list(scratch),
        compiler_params=pltpu.CompilerParams(vmem_limit_bytes=mib << 20),
        cost_estimate=pl.CostEstimate(flops=flops, bytes_accessed=nbytes, transcendentals=0),
    )


def tile_copies(tiles_ref, buf_ref, sems):
    n = tiles_ref.shape[0] // CHUNKS
    return [
        pltpu.make_async_copy(tiles_ref.at[pl.ds(c * n, n)], buf_ref.at[pl.ds(c * n, n)], sems.at[c])
        for c in range(CHUNKS)
    ]


def scatter_products(dest_ref, block_ref, src_ref, feats_ref, tiles_ref, out_ref, acc_ref, half_ref, buf_ref, sems, out_sems):
    copies = tile_copies(tiles_ref, buf_ref, sems)
    for c in copies:
        c.start()
    acc_ref[...] = jnp.zeros_like(acc_ref)
    n = tiles_ref.shape[0] // CHUNKS
    nblk = feats_ref.shape[1] // BLK
    for c in range(CHUNKS):
        copies[c].wait()
        for t in range(c * n, (c + 1) * n):
            col = pl.multiple_of(src_ref[t] * BLK, BLK)
            prod = lax.dot_general(
                feats_ref[:, pl.ds(col, BLK)],
                buf_ref[t],
                (((1,), (1,)), ((), ())),
                preferred_element_type=F32,
            )
            acc_ref[slot(dest_ref[t], block_ref[t], nblk)] += prod
    m = out_ref.shape[0] // CHUNKS
    writes = []
    for c in range(CHUNKS):
        part = pl.ds(c * m, m)
        half_ref[part] = acc_ref[part].astype(BF)
        writes.append(pltpu.make_async_copy(half_ref.at[part], out_ref.at[part], out_sems.at[c]))
        writes[c].start()
    for c in range(CHUNKS):
        writes[c].wait()


def gather_products(dest_ref, block_ref, src_ref, every_ref, tiles_ref, out_ref, acc_ref, buf_ref, sems):
    copies = tile_copies(tiles_ref, buf_ref, sems)
    for c in copies:
        c.start()
    acc_ref[...] = jnp.zeros_like(acc_ref)
    n = tiles_ref.shape[0] // CHUNKS
    nblk = acc_ref.shape[0]
    for c in range(CHUNKS):
        copies[c].wait()
        for t in range(c * n, (c + 1) * n):
            prod = jnp.dot(
                every_ref[slot(dest_ref[t], block_ref[t], nblk)], buf_ref[t], preferred_element_type=F32
            )
            acc_ref[src_ref[t]] += prod
    for b in range(nblk):
        out_ref[:, b * BLK : (b + 1) * BLK] = acc_ref[b].astype(BF)


def sum_first(got_ref, out_ref):
    total = got_ref[0].astype(F32)
    for k in range(1, got_ref.shape[0]):
        total += got_ref[k].astype(F32)
    out_ref[...] = total.astype(BF)


def finish_sum(got_ref, out_ref):
    for b in range(got_ref.shape[1]):
        total = got_ref[0, b].astype(F32)
        for k in range(1, got_ref.shape[0]):
            total += got_ref[k, b].astype(F32)
        total = total.astype(BF)
        for r in range(out_ref.shape[0]):
            out_ref[r, b] = total


def middle(rep_ref, got_ref, both_ref, hid_ref, msg_ref, wg_ref, all_ref, del_ref, mix_ref):
    reps, nblk, panel, _ = got_ref.shape
    rows = nblk * BLK
    for r in range(reps):
        for b in range(nblk):
            all_ref[r * panel : (r + 1) * panel, b * BLK : (b + 1) * BLK] = got_ref[r, b]
    own = pl.ds(pl.multiple_of(rep_ref[0] * panel, panel), panel)
    weight = both_ref[:, rows:]
    mixed = jnp.dot(weight, all_ref[...], preferred_element_type=F32)
    mix_ref[...] = mixed
    sig = jax.nn.sigmoid(mixed)
    delta = both_ref[:, :rows].astype(F32) * sig * (1.0 + mixed * (1.0 - sig))
    del_ref[...] = delta.astype(BF)
    mine = mix_ref[own, :]
    hid_ref[...] = (mine * jax.nn.sigmoid(mine)).astype(BF)
    mix_ref[...] = lax.dot_general(weight, del_ref[...], (((0,), (0,)), ((), ())), preferred_element_type=F32)
    sent = mix_ref[own, :].astype(BF)
    for z in range(msg_ref.shape[0]):
        for b in range(nblk):
            msg_ref[z, b] = sent[:, b * BLK : (b + 1) * BLK]
    wg_ref[...] = lax.dot_general(
        del_ref[own, :], all_ref[...], (((1,), (1,)), ((), ())), preferred_element_type=F32
    )


def spread(got_ref, msg_ref, sems):
    copies = [pltpu.make_async_copy(got_ref, msg_ref.at[k], sems.at[k]) for k in range(msg_ref.shape[0])]
    for c in copies:
        c.start()
    for c in copies:
        c.wait()


def per_device(feats, weight, tile_values, tile_dest, tile_block, tile_source, cotangent):
    panel, rows = feats.shape
    tiles = tile_values.shape[0]
    nblk = rows // BLK
    ntot = NY * NZ * nblk
    near = NY * NP
    reps = NX * NC
    full = reps * panel
    rep = lax.axis_index(("x", "core")).astype(jnp.int32).reshape(1)
    shape = jax.ShapeDtypeStruct
    tile_scratch = [pltpu.VMEM((tiles, BLK, BLK), BF), pltpu.SemaphoreType.DMA((CHUNKS,))]
    tile_bytes = tiles * BLK * BLK * 2
    tile_flops = 2 * tiles * panel * BLK * BLK
    places = tuple(map(in_hbm, (tile_dest[:, 0], tile_block, tile_source)))
    tile_values = in_hbm(tile_values)

    parts = call(
        scatter_products,
        "scatter_products",
        pltpu.HBM((ntot, panel, BLK), BF),
        [SMEM, SMEM, SMEM, VMEM, HBM],
        [
            pltpu.VMEM((ntot, panel, BLK), F32),
            pltpu.VMEM((ntot, panel, BLK), BF),
            *tile_scratch,
            pltpu.SemaphoreType.DMA((CHUNKS,)),
        ],
        flops=tile_flops,
        nbytes=tile_bytes,
        outs=HBM,
    )(*places, in_hbm(feats), tile_values)

    got = lax.all_to_all(parts.reshape(near, NZ8 * nblk, panel, BLK), ("y", "zp"), 0, 0)
    both = lax.all_gather(
        jnp.concatenate([cotangent, weight.T], axis=1), ("x", "core"), axis=0, tiled=True
    )
    got, both = lax.optimization_barrier((got, both))
    half = call(sum_first, "sum_near", shape((NZ8 * nblk, panel, BLK), BF), [VMEM], nbytes=ntot * panel * BLK * 2)(got)
    got = lax.all_to_all(half.reshape(NZ8, nblk, panel, BLK), "z8", 0, 0)
    mine = call(finish_sum, "sum_far", shape((reps, nblk, panel, BLK), BF), [VMEM], nbytes=1 << 19)(got)
    gathered = lax.all_to_all(mine, ("x", "core"), 0, 0)

    hidden, sent, wgrad = call(
        middle,
        "middle",
        (
            shape((panel, rows), BF),
            shape((NZ8, nblk, panel, BLK), BF),
            shape((panel, full), F32),
        ),
        [SMEM, VMEM, VMEM],
        [pltpu.VMEM((full, rows), BF), pltpu.VMEM((full, rows), BF), pltpu.VMEM((full, rows), F32)],
        flops=6 * full * full * rows,
        nbytes=1 << 20,
    )(rep, gathered, both)

    col = lax.all_to_all(sent, "z8", 0, 0)
    wsum = jnp.sum(lax.all_gather(wgrad, "y", axis=0), axis=0)
    col, wsum = lax.optimization_barrier((col, wsum))
    copies = call(
        spread,
        "spread",
        pltpu.HBM((near, NZ8 * nblk, panel, BLK), BF),
        [VMEM],
        [pltpu.SemaphoreType.DMA((near,))],
        nbytes=ntot * panel * BLK * 2,
        outs=HBM,
    )(col.reshape(NZ8 * nblk, panel, BLK))
    every = lax.all_to_all(copies, ("y", "zp"), 0, 0)
    wsum = jnp.sum(lax.all_gather(wsum, ("z8", "zp"), axis=0), axis=0)
    weight_grad = (wsum * float(rows * NY * NZ) ** (-0.5)).T
    every, weight_grad = lax.optimization_barrier((every, weight_grad))

    input_grad = call(
        gather_products,
        "gather_products",
        shape((panel, rows), BF),
        [SMEM, SMEM, SMEM, VMEM, HBM],
        [pltpu.VMEM((nblk, panel, BLK), F32), *tile_scratch],
        flops=tile_flops,
        nbytes=tile_bytes,
    )(*places, every.reshape(ntot, panel, BLK), tile_values)
    return hidden, weight_grad, input_grad


def solution(mesh):
    split = Mesh(mesh.devices.reshape(NY, NZ8, NP, NX, NC), ("y", "z8", "zp", "x", "core"))
    dom, rep = ("y", "z8", "zp"), ("x", "core")
    placed = (P(rep, dom), P(None, rep), P(dom, None, None), P(dom, None), P(dom), P(dom), P(rep, dom))
    return jax.shard_map(
        per_device,
        mesh=split,
        in_specs=placed,
        out_specs=(P(rep, dom), P(None, rep), P(rep, dom)),
        check_vma=False,
    )
```

time: 1180 us -> 173 us (0.15)
  the two profiles are of different devices: /device:TPU:4 before, /device:TPU:32 now
where the time goes in v2:
time: 173 us; the launch traced here: 172 us
  blocking collectives  108 us (62%)
  waiting for transfers between devices  25.5 us (15%)
  starting transfers between devices  22.2 us (13%)
  Pallas kernels  15.2 us (9%)
    all_gather x1, blocking collectives, per_device(): wsum = jnp.sum(lax.all_gather(wsum, ('z8', 'zp'), axis=0), axis=0)  49.2 us
    all_to_all x1, blocking collectives, per_device(): got = lax.all_to_all(half.reshape(NZ8, nblk, panel, BLK), 'z8', 0, 0)  33.6 us
    all_gather x1, blocking collectives, per_device(): lax.all_gather(jnp.concatenate([cotangent, weight.T], axis=1), ('x', 'cor...  13 us
    all_gather x1, blocking collectives, per_device(): wsum = jnp.sum(lax.all_gather(wgrad, 'y', axis=0), axis=0)  12.1 us
    all_to_all x1, waiting for transfers between devices, per_device(): lax.all_to_all(parts.reshape(near, NZ8 * nblk, panel, BLK), ('y', 'zp'),...  9.71 us
    all_to_all x1, starting transfers between devices, per_device(): lax.all_to_all(parts.reshape(near, NZ8 * nblk, panel, BLK), ('y', 'zp'),...  9.01 us
    all_to_all x1, waiting for transfers between devices, per_device(): col = lax.all_to_all(sent, 'z8', 0, 0)  8.28 us
    all_to_all x1, waiting for transfers between devices, per_device(): gathered = lax.all_to_all(mine, ('x', 'core'), 0, 0)  7.54 us
  transfers between devices with their start and end apart: 4, of which 3 were waited for; matrix products, arithmetic and copies ran while one was open for 0% of the time, Pallas kernels for 0%

profile of v2, /device:TPU:32, one launch (start us, length us, event | category | flops | bytes accessed | tf_op | source)
XLA Modules:
  0.0 172.2 jit_solution(17723769343508369173)
XLA Ops:
  0.6 6.5 %scatter_products.1 = bf16[256,32,128]{2,1,0:T(8,128)(2,1)} custom-call(s32[128]{0:T(128)} %bitcast.18, s32[128]{0:T(128)} %block_ref.3, s32[128]{0:T(128)} %src_ref.3, bf16[32,512]{1,0:T(8,128)(2,1)} %feats_ref.1, bf16[128,128,128]{2,1,0:T(8,128)(2,1)} %tiles_ref.3), custom_call_target="tpu_custom_call" | custom-call | flops 134217728 | bytes 4194304 | tf_op jit(solution)/shard_map/scatter_products/pallas_call | solution.py:164
  7.1 0.0 copy-start
  7.1 0.0 copy-start.1
  7.1 9.0 %all-to-all-start = ((bf16[8,32,32,128]{3,2,1,0:T(8,128)(2,1)}), bf16[8,32,32,128]{3,2,1,0:T(8,128)(2,1)S(1)}, u32[]{:S(2)}, u32[]{:S(2)}) async-start(bf16[8,32,32,128]{3,2,1,0:T(8,128)(2,1)} %bitcast.14), calls=%async_computation | async-start | bytes 4194304 | tf_op jit(solution)/shard_map/all_to_all | solution.py:180
  16.1 0.0 copy-done
  16.1 0.0 copy-done.1
  16.2 13.0 %all_gather.15.both_ref = bf16[256,768]{1,0:T(8,128)(2,1)S(1)} all-gather(bf16[32,768]{1,0:T(8,128)(2,1)S(1)} %pad_maximum_fusion), channel_id=1, replica_groups=mesh['y'=4,'z8'=8,'zp'=2,'x'=4,'core'=2] {'x','core'}, dimensions={0}, use_global_device_ids=true | all-gather | bytes 442368 | tf_op jit(solution)/shard_map/all_gather | solution.py:181
  29.1 9.7 %all-to-all-done.got_ref = bf16[8,32,32,128]{3,2,1,0:T(8,128)(2,1)S(1)} async-done(((bf16[8,32,32,128]{3,2,1,0:T(8,128)(2,1)}), bf16[8,32,32,128]{3,2,1,0:T(8,128)(2,1)S(1)}, u32[]{:S(2)}, u32[]{:S(2)}) %all-to-all-start) | async-done | bytes 2097184 | tf_op jit(solution)/shard_map/all_to_all | solution.py:180
  38.8 0.3 sum_near.1
  39.1 33.6 %all_to_all.25.got_ref = bf16[8,4,32,128]{3,2,1,0:T(8,128)(2,1)S(1)} all-to-all(bf16[8,4,32,128]{3,2,1,0:T(8,128)(2,1)S(1)} %bitcast.13), channel_id=1, replica_groups=mesh['y'=4,'z8'=8,'zp'=2,'x'=4,'core'=2] {'z8'}, dimensions={0} | all-to-all | bytes 524288 | tf_op jit(solution)/shard_map/all_to_all | solution.py:186
  72.7 0.7 sum_far.1
  73.5 4.3 %all-to-all-start.2 = ((bf16[8,4,32,128]{3,2,1,0:T(8,128)(2,1)}), bf16[8,4,32,128]{3,2,1,0:T(8,128)(2,1)S(1)}, u32[]{:S(2)}, u32[]{:S(2)}) async-start(bf16[8,4,32,128]{3,2,1,0:T(8,128)(2,1)} %sum_far.1), calls=%async_computation.2 | async-start | bytes 524288 | tf_op jit(solution)/shard_map/all_to_all | solution.py:188
  77.8 7.5 %all-to-all-done.2.got_ref = bf16[8,4,32,128]{3,2,1,0:T(8,128)(2,1)S(1)} async-done(((bf16[8,4,32,128]{3,2,1,0:T(8,128)(2,1)}), bf16[8,4,32,128]{3,2,1,0:T(8,128)(2,1)S(1)}, u32[]{:S(2)}, u32[]{:S(2)}) %all-to-all-start.2) | async-done | bytes 262176 | tf_op jit(solution)/shard_map/all_to_all | solution.py:188
  85.3 1.3 middle.1
  86.6 3.4 %all-to-all-start.3 = ((bf16[8,4,32,128]{3,2,1,0:T(8,128)(2,1)}), bf16[8,4,32,128]{3,2,1,0:T(8,128)(2,1)S(1)}, u32[]{:S(2)}, u32[]{:S(2)}) async-start(bf16[8,4,32,128]{3,2,1,0:T(8,128)(2,1)} %get-tuple-element.15), calls=%async_computation.3 | async-start | bytes 524288 | tf_op jit(solution)/shard_map/all_to_all | solution.py:204
  90.0 12.1 %all-gather = f32[128,256]{1,0:T(8,128)S(1)} all-gather(f32[32,256]{1,0:T(8,128)S(1)} %get-tuple-element.16), channel_id=2, replica_groups=mesh['y'=4,'z8'=8,'zp'=2,'x'=4,'core'=2] {'y'}, dimensions={0}, use_global_device_ids=true | all-gather | bytes 163840 | tf_op jit(solution)/shard_map/all_gather | solution.py:205
  102.1 8.3 %all-to-all-done.3 = bf16[8,4,32,128]{3,2,1,0:T(8,128)(2,1)S(1)} async-done(((bf16[8,4,32,128]{3,2,1,0:T(8,128)(2,1)}), bf16[8,4,32,128]{3,2,1,0:T(8,128)(2,1)S(1)}, u32[]{:S(2)}, u32[]{:S(2)}) %all-to-all-start.3) | async-done | bytes 262176 | tf_op jit(solution)/shard_map/all_to_all | solution.py:204
  110.4 1.4 spread.1
  111.8 5.4 %all-to-all-start.4 = ((bf16[8,32,32,128]{3,2,1,0:T(8,128)(2,1)}), bf16[8,32,32,128]{3,2,1,0:T(8,128)(2,1)S(1)}, u32[]{:S(2)}, u32[]{:S(2)}) async-start(bf16[8,32,32,128]{3,2,1,0:T(8,128)(2,1)} %spread.1), calls=%async_computation.4 | async-start | bytes 4194304 | tf_op jit(solution)/shard_map/all_to_all | solution.py:216
  117.3 49.2 %all-gather.1 = f32[512,256]{1,0:T(8,128)S(1)} all-gather(f32[32,256]{1,0:T(8,128)S(1)} %reduce_sum.18), channel_id=3, replica_groups=mesh['y'=4,'z8'=8,'zp'=2,'x'=4,'core'=2] {'z8','zp'}, dimensions={0}, use_global_device_ids=true | all-gather | bytes 557056 | tf_op jit(solution)/shard_map/all_gather | solution.py:217
  166.5 0.6 multiply_bitcast_fusion
  167.1 0.0 all-to-all-done.4
  167.1 5.0 %gather_products.1 = bf16[32,512]{1,0:T(8,128)(2,1)} custom-call(s32[128]{0:T(128)} %bitcast.19, s32[128]{0:T(128)} %block_ref.3, s32[128]{0:T(128)} %src_ref.3, bf16[256,32,128]{2,1,0:T(8,128)(2,1)S(1)} %bitcast.11, bf16[128,128,128]{2,1,0:T(8,128)(2,1)} %tiles_ref.3), custom_call_target="tpu_custom_call" | custom-call | flops 134217728 | bytes 4194304 | tf_op jit(solution)/shard_map/gather_products/pallas_call | solution.py:221
  (3 shorter events, 0.1 us)
Async XLA Ops:
  7.1 9.0 %copy-start = (bf16[32,512]{1,0:T(8,128)(2,1)S(1)}, bf16[32,512]{1,0:T(8,128)(2,1)}, u32[]{:S(2)}) copy-start(bf16[32,512]{1,0:T(8,128)(2,1)} %param.13) | copy-start | bytes 98308
  7.1 9.0 %copy-start.1 = (bf16[256,32]{0,1:T(8,128)(2,1)S(1)}, bf16[256,32]{0,1:T(8,128)(2,1)}, u32[]{:S(2)}) copy-start(bf16[256,32]{0,1:T(8,128)(2,1)} %param.8) | copy-start | bytes 49156
  7.1 31.7 %all-to-all-start = ((bf16[8,32,32,128]{3,2,1,0:T(8,128)(2,1)}), bf16[8,32,32,128]{3,2,1,0:T(8,128)(2,1)S(1)}, u32[]{:S(2)}, u32[]{:S(2)}) async-start(bf16[8,32,32,128]{3,2,1,0:T(8,128)(2,1)} %bitcast.14), calls=%async_computation | async-start | bytes 4194304 | tf_op jit(solution)/shard_map/all_to_all | solution.py:180
  73.5 11.8 %all-to-all-start.2 = ((bf16[8,4,32,128]{3,2,1,0:T(8,128)(2,1)}), bf16[8,4,32,128]{3,2,1,0:T(8,128)(2,1)S(1)}, u32[]{:S(2)}, u32[]{:S(2)}) async-start(bf16[8,4,32,128]{3,2,1,0:T(8,128)(2,1)} %sum_far.1), calls=%async_computation.2 | async-start | bytes 524288 | tf_op jit(solution)/shard_map/all_to_all | solution.py:188
  86.6 23.8 %all-to-all-start.3 = ((bf16[8,4,32,128]{3,2,1,0:T(8,128)(2,1)}), bf16[8,4,32,128]{3,2,1,0:T(8,128)(2,1)S(1)}, u32[]{:S(2)}, u32[]{:S(2)}) async-start(bf16[8,4,32,128]{3,2,1,0:T(8,128)(2,1)} %get-tuple-element.15), calls=%async_computation.3 | async-start | bytes 524288 | tf_op jit(solution)/shard_map/all_to_all | solution.py:204
  111.8 55.3 %all-to-all-start.4 = ((bf16[8,32,32,128]{3,2,1,0:T(8,128)(2,1)}), bf16[8,32,32,128]{3,2,1,0:T(8,128)(2,1)S(1)}, u32[]{:S(2)}, u32[]{:S(2)}) async-start(bf16[8,32,32,128]{3,2,1,0:T(8,128)(2,1)} %spread.1), calls=%async_computation.4 | async-start | bytes 4194304 | tf_op jit(solution)/shard_map/all_to_all | solution.py:216

commit v3 on v2

--- a/solution.py
+++ b/solution.py
@@ -21,9 +21,9 @@
     return pltpu.with_memory_space_constraint(x, pltpu.HBM)
 
 
-def slot(dest, block, nblk):
-    y, z = dest // NZ, dest % NZ
-    return (((y * NP) + z % NP) * NZ8 + z // NP) * nblk + block
+def slot(dest, block, nblk, stride):
+    near = lax.shift_right_logical(dest, 4) * NP + (dest & (NP - 1))
+    return near * stride + (lax.shift_right_logical(dest, 1) & (NZ8 - 1)) * nblk + block
 
 
 def call(kernel, name, out_shape, in_specs, scratch=(), mib=24, flops=0, nbytes=0, outs=None):
@@ -65,7 +65,7 @@
                 (((1,), (1,)), ((), ())),
                 preferred_element_type=F32,
             )
-            acc_ref[slot(dest_ref[t], block_ref[t], nblk)] += prod
+            acc_ref[slot(dest_ref[t], block_ref[t], nblk, NZ8 * nblk)] += prod
     m = out_ref.shape[0] // CHUNKS
     writes = []
     for c in range(CHUNKS):
@@ -77,18 +77,24 @@
         writes[c].wait()
 
 
-def gather_products(dest_ref, block_ref, src_ref, every_ref, tiles_ref, out_ref, acc_ref, buf_ref, sems):
+def gather_products(dest_ref, block_ref, src_ref, every_ref, tiles_ref, out_ref, wg_ref, acc_ref, buf_ref, sems):
     copies = tile_copies(tiles_ref, buf_ref, sems)
     for c in copies:
         c.start()
     acc_ref[...] = jnp.zeros_like(acc_ref)
     n = tiles_ref.shape[0] // CHUNKS
-    nblk = acc_ref.shape[0]
+    nblk, panel, _ = acc_ref.shape
+    stride = every_ref.shape[0] // (NY * NP)
+    for h in range(stride - NZ8 * nblk):
+        total = jnp.zeros((panel, BLK), F32)
+        for k in range(NY * NP):
+            total += every_ref[k * stride + NZ8 * nblk + h].astype(F32)
+        wg_ref[:, h * BLK : (h + 1) * BLK] = total * float(nblk * BLK * NY * NZ) ** (-0.5)
     for c in range(CHUNKS):
         copies[c].wait()
         for t in range(c * n, (c + 1) * n):
             prod = jnp.dot(
-                every_ref[slot(dest_ref[t], block_ref[t], nblk)], buf_ref[t], preferred_element_type=F32
+                every_ref[slot(dest_ref[t], block_ref[t], nblk, stride)], buf_ref[t], preferred_element_type=F32
             )
             acc_ref[src_ref[t]] += prod
     for b in range(nblk):
@@ -112,12 +118,12 @@
             out_ref[r, b] = total
 
 
-def middle(rep_ref, got_ref, both_ref, hid_ref, msg_ref, wg_ref, all_ref, del_ref, mix_ref):
-    reps, nblk, panel, _ = got_ref.shape
+def middle(rep_ref, got_ref, both_ref, hid_ref, msg_ref, all_ref, del_ref, mix_ref):
+    cores, chips, nblk, panel, _ = got_ref.shape
     rows = nblk * BLK
-    for r in range(reps):
+    for r in range(cores * chips):
         for b in range(nblk):
-            all_ref[r * panel : (r + 1) * panel, b * BLK : (b + 1) * BLK] = got_ref[r, b]
+            all_ref[r * panel : (r + 1) * panel, b * BLK : (b + 1) * BLK] = got_ref[r % cores, r // cores, b]
     own = pl.ds(pl.multiple_of(rep_ref[0] * panel, panel), panel)
     weight = both_ref[:, rows:]
     mixed = jnp.dot(weight, all_ref[...], preferred_element_type=F32)
@@ -129,16 +135,27 @@
     hid_ref[...] = (mine * jax.nn.sigmoid(mine)).astype(BF)
     mix_ref[...] = lax.dot_general(weight, del_ref[...], (((0,), (0,)), ((), ())), preferred_element_type=F32)
     sent = mix_ref[own, :].astype(BF)
+    wgrad = lax.dot_general(
+        del_ref[own, :], all_ref[...], (((1,), (1,)), ((), ())), preferred_element_type=F32
+    ).astype(BF)
     for z in range(msg_ref.shape[0]):
         for b in range(nblk):
             msg_ref[z, b] = sent[:, b * BLK : (b + 1) * BLK]
-    wg_ref[...] = lax.dot_general(
-        del_ref[own, :], all_ref[...], (((1,), (1,)), ((), ())), preferred_element_type=F32
-    )
-
-
-def spread(got_ref, msg_ref, sems):
-    copies = [pltpu.make_async_copy(got_ref, msg_ref.at[k], sems.at[k]) for k in range(msg_ref.shape[0])]
+        for h in range(msg_ref.shape[1] - nblk):
+            msg_ref[z, nblk + h] = wgrad[:, h * BLK : (h + 1) * BLK]
+
+
+def spread(got_ref, msg_ref, one_ref, sems):
+    pairs, blocks, panel, _ = got_ref.shape
+    nblk = (one_ref.shape[0] - blocks) // (pairs - 1)
+    for z in range(pairs):
+        one_ref[z * nblk : (z + 1) * nblk] = got_ref[z, :nblk]
+    for h in range(blocks - nblk):
+        total = jnp.zeros((panel, BLK), F32)
+        for z in range(pairs):
+            total += got_ref[z, nblk + h].astype(F32)
+        one_ref[pairs * nblk + h] = total.astype(BF)
+    copies = [pltpu.make_async_copy(one_ref, msg_ref.at[k], sems.at[k]) for k in range(msg_ref.shape[0])]
     for c in copies:
         c.start()
     for c in copies:
@@ -151,8 +168,9 @@
     nblk = rows // BLK
     ntot = NY * NZ * nblk
     near = NY * NP
-    reps = NX * NC
-    full = reps * panel
+    full = NX * NC * panel
+    halves = full // BLK
+    stride = NZ8 * nblk + halves
     rep = lax.axis_index(("x", "core")).astype(jnp.int32).reshape(1)
     shape = jax.ShapeDtypeStruct
     tile_scratch = [pltpu.VMEM((tiles, BLK, BLK), BF), pltpu.SemaphoreType.DMA((CHUNKS,))]
@@ -184,16 +202,15 @@
     got, both = lax.optimization_barrier((got, both))
     half = call(sum_first, "sum_near", shape((NZ8 * nblk, panel, BLK), BF), [VMEM], nbytes=ntot * panel * BLK * 2)(got)
     got = lax.all_to_all(half.reshape(NZ8, nblk, panel, BLK), "z8", 0, 0)
-    mine = call(finish_sum, "sum_far", shape((reps, nblk, panel, BLK), BF), [VMEM], nbytes=1 << 19)(got)
-    gathered = lax.all_to_all(mine, ("x", "core"), 0, 0)
-
-    hidden, sent, wgrad = call(
+    mine = call(finish_sum, "sum_far", shape((NX, nblk, panel, BLK), BF), [VMEM], nbytes=1 << 19)(got)
+    gathered = lax.all_gather(lax.all_to_all(mine, "x", 0, 0), "core", axis=0)
+
+    hidden, sent = call(
         middle,
         "middle",
         (
             shape((panel, rows), BF),
-            shape((NZ8, nblk, panel, BLK), BF),
-            shape((panel, full), F32),
+            shape((NZ8, nblk + halves, panel, BLK), BF),
         ),
         [SMEM, VMEM, VMEM],
         [pltpu.VMEM((full, rows), BF), pltpu.VMEM((full, rows), BF), pltpu.VMEM((full, rows), F32)],
@@ -202,32 +219,27 @@
     )(rep, gathered, both)
 
     col = lax.all_to_all(sent, "z8", 0, 0)
-    wsum = jnp.sum(lax.all_gather(wgrad, "y", axis=0), axis=0)
-    col, wsum = lax.optimization_barrier((col, wsum))
     copies = call(
         spread,
         "spread",
-        pltpu.HBM((near, NZ8 * nblk, panel, BLK), BF),
+        pltpu.HBM((near, stride, panel, BLK), BF),
         [VMEM],
-        [pltpu.SemaphoreType.DMA((near,))],
+        [pltpu.VMEM((stride, panel, BLK), BF), pltpu.SemaphoreType.DMA((near,))],
         nbytes=ntot * panel * BLK * 2,
         outs=HBM,
-    )(col.reshape(NZ8 * nblk, panel, BLK))
+    )(col)
     every = lax.all_to_all(copies, ("y", "zp"), 0, 0)
-    wsum = jnp.sum(lax.all_gather(wsum, ("z8", "zp"), axis=0), axis=0)
-    weight_grad = (wsum * float(rows * NY * NZ) ** (-0.5)).T
-    every, weight_grad = lax.optimization_barrier((every, weight_grad))
-
-    input_grad = call(
+
+    input_grad, weight_grad = call(
         gather_products,
         "gather_products",
-        shape((panel, rows), BF),
+        (shape((panel, rows), BF), shape((panel, full), F32)),
         [SMEM, SMEM, SMEM, VMEM, HBM],
         [pltpu.VMEM((nblk, panel, BLK), F32), *tile_scratch],
         flops=tile_flops,
         nbytes=tile_bytes,
-    )(*places, every.reshape(ntot, panel, BLK), tile_values)
-    return hidden, weight_grad, input_grad
+    )(*places, every.reshape(near * stride, panel, BLK), tile_values)
+    return hidden, weight_grad.T, input_grad
 
 
 def solution(mesh):

time: 173 us -> 157 us (0.908)
  the two profiles are of different devices: /device:TPU:32 before, /device:TPU:1 now
where the time goes in v3:
time: 157 us; the launch traced here: 156 us
  blocking collectives  120 us (76%)
  Pallas kernels  14.4 us (9%)
  waiting for transfers between devices  10.9 us (7%)
  starting transfers between devices  10.4 us (7%)
    all_to_all x1, blocking collectives, per_device(): got = lax.all_to_all(half.reshape(NZ8, nblk, panel, BLK), 'z8', 0, 0)  34.3 us
    all_to_all x1, blocking collectives, per_device(): every = lax.all_to_all(copies, ('y', 'zp'), 0, 0)  32 us
    all_to_all x1, blocking collectives, per_device(): col = lax.all_to_all(sent, 'z8', 0, 0)  28.7 us
    all_gather x1, blocking collectives, per_device(): lax.all_gather(jnp.concatenate([cotangent, weight.T], axis=1), ('x', 'cor...  16.9 us
    all_gather x1, blocking collectives, per_device(): gathered = lax.all_gather(lax.all_to_all(mine, 'x', 0, 0), 'core', axis=0)  7.62 us
    pallas_call x1, Pallas kernels, per_device(): call(scatter_products, 'scatter_products', pltpu.HBM((ntot, panel, BLK),...  6.49 us
    all_to_all x1, starting transfers between devices, per_device(): lax.all_to_all(parts.reshape(near, NZ8 * nblk, panel, BLK), ('y', 'zp'),...  6.39 us
    all_to_all x1, waiting for transfers between devices, per_device(): lax.all_to_all(parts.reshape(near, NZ8 * nblk, panel, BLK), ('y', 'zp'),...  6.05 us
  transfers between devices with their start and end apart: 2, of which 2 were waited for; matrix products, arithmetic and copies ran while one was open for 0% of the time, Pallas kernels for 0%

profile of v3, /device:TPU:1, one launch (start us, length us, event | category | flops | bytes accessed | tf_op | source)
XLA Modules:
  0.0 156.0 jit_solution(4245993431688053820)
XLA Ops:
  0.6 6.5 %scatter_products.1 = bf16[256,32,128]{2,1,0:T(8,128)(2,1)} custom-call(s32[128]{0:T(128)} %bitcast.13, s32[128]{0:T(128)} %block_ref.3, s32[128]{0:T(128)} %src_ref.3, bf16[32,512]{1,0:T(8,128)(2,1)} %feats_ref.1, bf16[128,128,128]{2,1,0:T(8,128)(2,1)} %tiles_ref.3), custom_call_target="tpu_custom_call" | custom-call | flops 134217728 | bytes 4194304 | tf_op jit(solution)/shard_map/scatter_products/pallas_call | solution.py:182
  7.1 0.0 copy-start
  7.1 0.0 copy-start.1
  7.1 6.4 %all-to-all-start = ((bf16[8,32,32,128]{3,2,1,0:T(8,128)(2,1)}), bf16[8,32,32,128]{3,2,1,0:T(8,128)(2,1)S(1)}, u32[]{:S(2)}, u32[]{:S(2)}) async-start(bf16[8,32,32,128]{3,2,1,0:T(8,128)(2,1)} %bitcast.11), calls=%async_computation | async-start | bytes 4194304 | tf_op jit(solution)/shard_map/all_to_all | solution.py:198
  13.5 0.0 copy-done
  13.5 0.0 copy-done.1
  13.6 16.9 %all_gather.9.both_ref = bf16[256,768]{1,0:T(8,128)(2,1)S(1)} all-gather(bf16[32,768]{1,0:T(8,128)(2,1)S(1)} %pad_maximum_fusion), channel_id=1, replica_groups=mesh['y'=4,'z8'=8,'zp'=2,'x'=4,'core'=2] {'x','core'}, dimensions={0}, use_global_device_ids=true | all-gather | bytes 442368 | tf_op jit(solution)/shard_map/all_gather | solution.py:199
  30.5 6.1 %all-to-all-done.got_ref = bf16[8,32,32,128]{3,2,1,0:T(8,128)(2,1)S(1)} async-done(((bf16[8,32,32,128]{3,2,1,0:T(8,128)(2,1)}), bf16[8,32,32,128]{3,2,1,0:T(8,128)(2,1)S(1)}, u32[]{:S(2)}, u32[]{:S(2)}) %all-to-all-start) | async-done | bytes 2097184 | tf_op jit(solution)/shard_map/all_to_all | solution.py:198
  36.5 0.3 sum_near.1
  36.8 34.3 %all_to_all.25.got_ref = bf16[8,4,32,128]{3,2,1,0:T(8,128)(2,1)S(1)} all-to-all(bf16[8,4,32,128]{3,2,1,0:T(8,128)(2,1)S(1)} %bitcast.9), channel_id=1, replica_groups=mesh['y'=4,'z8'=8,'zp'=2,'x'=4,'core'=2] {'z8'}, dimensions={0} | all-to-all | bytes 524288 | tf_op jit(solution)/shard_map/all_to_all | solution.py:204
  71.2 0.7 sum_far.1
  71.8 4.0 %all-to-all-start.2 = ((bf16[4,4,32,128]{3,2,1,0:T(8,128)(2,1)}), bf16[4,4,32,128]{3,2,1,0:T(8,128)(2,1)S(1)}, u32[]{:S(2)}, u32[]{:S(2)}) async-start(bf16[4,4,32,128]{3,2,1,0:T(8,128)(2,1)} %sum_far.1), calls=%async_computation.2 | async-start | bytes 262144 | tf_op jit(solution)/shard_map/all_to_all | solution.py:206
  75.9 4.8 %all-to-all-done.2 = bf16[4,4,32,128]{3,2,1,0:T(8,128)(2,1)S(1)} async-done(((bf16[4,4,32,128]{3,2,1,0:T(8,128)(2,1)}), bf16[4,4,32,128]{3,2,1,0:T(8,128)(2,1)S(1)}, u32[]{:S(2)}, u32[]{:S(2)}) %all-to-all-start.2) | async-done | bytes 131104 | tf_op jit(solution)/shard_map/all_to_all | solution.py:206
  80.7 7.6 %all-gather = bf16[8,4,32,128]{3,2,1,0:T(8,128)(2,1)S(1)} all-gather(bf16[4,4,32,128]{3,2,1,0:T(8,128)(2,1)S(1)} %all-to-all-done.2), channel_id=2, replica_groups=mesh['y'=4,'z8'=8,'zp'=2,'x'=4,'core'=2] {'core'}, dimensions={0}, use_global_device_ids=true | all-gather | bytes 393216 | tf_op jit(solution)/shard_map/all_gather | solution.py:206
  88.3 1.0 middle.1
  89.3 28.7 %all_to_all.26.got_ref = bf16[8,6,32,128]{3,2,1,0:T(8,128)(2,1)S(1)} all-to-all(bf16[8,6,32,128]{3,2,1,0:T(8,128)(2,1)S(1)} %get-tuple-element.12), channel_id=1, replica_groups=mesh['y'=4,'z8'=8,'zp'=2,'x'=4,'core'=2] {'z8'}, dimensions={0} | all-to-all | bytes 786432 | tf_op jit(solution)/shard_map/all_to_all | solution.py:221
  118.0 1.5 spread.1
  119.5 32.0 %all_to_all.27 = bf16[8,34,32,128]{3,2,1,0:T(8,128)(2,1)S(1)} all-to-all(bf16[8,34,32,128]{3,2,1,0:T(8,128)(2,1)} %spread.1), channel_id=1, replica_groups=mesh['y'=4,'z8'=8,'zp'=2,'x'=4,'core'=2] {'y','zp'}, dimensions={0} | all-to-all | bytes 4456448 | tf_op jit(solution)/shard_map/all_to_all | solution.py:231
  151.5 4.5 %gather_products.1 = (bf16[32,512]{1,0:T(8,128)(2,1)}, f32[32,256]{1,0:T(8,128)}) custom-call(s32[128]{0:T(128)} %bitcast.14, s32[128]{0:T(128)} %block_ref.3, s32[128]{0:T(128)} %src_ref.3, bf16[272,32,128]{2,1,0:T(8,128)(2,1)S(1)} %bitcast.8, bf16[128,128,128]{2,1,0:T(8,128)(2,1)} %tiles_ref.3), custom_call_target="tpu_custom_call" | custom-call | flops 134217728 | bytes 4194304 | tf_op jit(solution)/shard_map/gather_products/pallas_call | solution.py:233
  (1 shorter events, 0.0 us)
Async XLA Ops:
  7.1 6.4 %copy-start = (bf16[32,512]{1,0:T(8,128)(2,1)S(1)}, bf16[32,512]{1,0:T(8,128)(2,1)}, u32[]{:S(2)}) copy-start(bf16[32,512]{1,0:T(8,128)(2,1)} %param.13) | copy-start | bytes 98308
  7.1 6.4 %copy-start.1 = (bf16[256,32]{0,1:T(8,128)(2,1)S(1)}, bf16[256,32]{0,1:T(8,128)(2,1)}, u32[]{:S(2)}) copy-start(bf16[256,32]{0,1:T(8,128)(2,1)} %param.8) | copy-start | bytes 49156
  7.1 29.4 %all-to-all-start = ((bf16[8,32,32,128]{3,2,1,0:T(8,128)(2,1)}), bf16[8,32,32,128]{3,2,1,0:T(8,128)(2,1)S(1)}, u32[]{:S(2)}, u32[]{:S(2)}) async-start(bf16[8,32,32,128]{3,2,1,0:T(8,128)(2,1)} %bitcast.11), calls=%async_computation | async-start | bytes 4194304 | tf_op jit(solution)/shard_map/all_to_all | solution.py:198
  71.8 8.8 %all-to-all-start.2 = ((bf16[4,4,32,128]{3,2,1,0:T(8,128)(2,1)}), bf16[4,4,32,128]{3,2,1,0:T(8,128)(2,1)S(1)}, u32[]{:S(2)}, u32[]{:S(2)}) async-start(bf16[4,4,32,128]{3,2,1,0:T(8,128)(2,1)} %sum_far.1), calls=%async_computation.2 | async-start | bytes 262144 | tf_op jit(solution)/shard_map/all_to_all | solution.py:206

commit v4 on v3

--- a/solution.py
+++ b/solution.py
@@ -1,5 +1,8 @@
+import math
+
 import jax
 import jax.numpy as jnp
+import numpy as np
 from jax import lax
 from jax.experimental import pallas as pl
 from jax.experimental.pallas import tpu as pltpu
@@ -9,7 +12,8 @@
 F32 = jnp.float32
 NY, NZ, NX, NC = 4, 16, 4, 2
 BLK = 128
-CHUNKS = 8
+CHUNKS = (16, 48, 64)
+WRITES = 4
 NZ8, NP = NZ // 2, 2
 
 SMEM = pl.BlockSpec(memory_space=pltpu.SMEM)
@@ -21,9 +25,28 @@
     return pltpu.with_memory_space_constraint(x, pltpu.HBM)
 
 
+AXES = ("y", "z8", "zp", "x", "core")
+SIZES = (NY, NZ8, NP, NX, NC)
+NEAR_ORDER = [(0, 0), (1, 0), (2, 0), (3, 0), (0, 1), (1, 1), (2, 1), (3, 1)]
+FAR_ORDER = [(0,), (4,), (2,), (6,), (1,), (5,), (3,), (7,)]
+X_ORDER = [(0,), (2,), (1,), (3,)]
+
+
+def exchange(x, axes, order):
+    others = [a for a in AXES if a not in axes]
+    ranks = np.arange(math.prod(SIZES)).reshape(SIZES)
+    ranks = ranks.transpose([AXES.index(a) for a in (*others, *axes)])
+    ranks = ranks.reshape(-1, *(SIZES[AXES.index(a)] for a in axes))
+    groups = [[int(r[m]) for m in order] for r in ranks]
+    flat = x.reshape(x.shape[0], -1, BLK)
+    return lax.all_to_all(flat, AXES, 0, 0, tiled=True, axis_index_groups=groups).reshape(x.shape)
+
+
 def slot(dest, block, nblk, stride):
-    near = lax.shift_right_logical(dest, 4) * NP + (dest & (NP - 1))
-    return near * stride + (lax.shift_right_logical(dest, 1) & (NZ8 - 1)) * nblk + block
+    y, z = lax.shift_right_logical(dest, 4), dest & 15
+    near = (z & 1) * 4 + y
+    far = (z & 2) * 2 + lax.shift_right_logical(z & 4, 1) + lax.shift_right_logical(z, 3)
+    return near * stride + far * nblk + block
 
 
 def call(kernel, name, out_shape, in_specs, scratch=(), mib=24, flops=0, nbytes=0, outs=None):
@@ -40,24 +63,19 @@
     )
 
 
-def tile_copies(tiles_ref, buf_ref, sems):
-    n = tiles_ref.shape[0] // CHUNKS
-    return [
-        pltpu.make_async_copy(tiles_ref.at[pl.ds(c * n, n)], buf_ref.at[pl.ds(c * n, n)], sems.at[c])
-        for c in range(CHUNKS)
-    ]
-
-
-def scatter_products(dest_ref, block_ref, src_ref, feats_ref, tiles_ref, out_ref, acc_ref, half_ref, buf_ref, sems, out_sems):
-    copies = tile_copies(tiles_ref, buf_ref, sems)
-    for c in copies:
-        c.start()
+def scatter_products(
+    dest_ref, block_ref, src_ref, feats_ref, tiles_ref, out_ref, acc_ref, half_ref, buf_ref, sems, out_sems
+):
+    copies = []
+    for c, n in enumerate(CHUNKS):
+        part = pl.ds(sum(CHUNKS[:c]), n)
+        copies.append(pltpu.make_async_copy(tiles_ref.at[part], buf_ref.at[part], sems.at[c]))
+        copies[c].start()
     acc_ref[...] = jnp.zeros_like(acc_ref)
-    n = tiles_ref.shape[0] // CHUNKS
     nblk = feats_ref.shape[1] // BLK
-    for c in range(CHUNKS):
+    for c, n in enumerate(CHUNKS):
         copies[c].wait()
-        for t in range(c * n, (c + 1) * n):
+        for t in range(sum(CHUNKS[:c]), sum(CHUNKS[:c]) + n):
             col = pl.multiple_of(src_ref[t] * BLK, BLK)
             prod = lax.dot_general(
                 feats_ref[:, pl.ds(col, BLK)],
@@ -66,23 +84,19 @@
                 preferred_element_type=F32,
             )
             acc_ref[slot(dest_ref[t], block_ref[t], nblk, NZ8 * nblk)] += prod
-    m = out_ref.shape[0] // CHUNKS
+    m = out_ref.shape[0] // WRITES
     writes = []
-    for c in range(CHUNKS):
+    for c in range(WRITES):
         part = pl.ds(c * m, m)
         half_ref[part] = acc_ref[part].astype(BF)
         writes.append(pltpu.make_async_copy(half_ref.at[part], out_ref.at[part], out_sems.at[c]))
         writes[c].start()
-    for c in range(CHUNKS):
+    for c in range(WRITES):
         writes[c].wait()
 
 
-def gather_products(dest_ref, block_ref, src_ref, every_ref, tiles_ref, out_ref, wg_ref, acc_ref, buf_ref, sems):
-    copies = tile_copies(tiles_ref, buf_ref, sems)
-    for c in copies:
-        c.start()
+def gather_products(dest_ref, block_ref, src_ref, every_ref, tiles_ref, out_ref, wg_ref, acc_ref):
     acc_ref[...] = jnp.zeros_like(acc_ref)
-    n = tiles_ref.shape[0] // CHUNKS
     nblk, panel, _ = acc_ref.shape
     stride = every_ref.shape[0] // (NY * NP)
     for h in range(stride - NZ8 * nblk):
@@ -90,13 +104,11 @@
         for k in range(NY * NP):
             total += every_ref[k * stride + NZ8 * nblk + h].astype(F32)
         wg_ref[:, h * BLK : (h + 1) * BLK] = total * float(nblk * BLK * NY * NZ) ** (-0.5)
-    for c in range(CHUNKS):
-        copies[c].wait()
-        for t in range(c * n, (c + 1) * n):
-            prod = jnp.dot(
-                every_ref[slot(dest_ref[t], block_ref[t], nblk, stride)], buf_ref[t], preferred_element_type=F32
-            )
-            acc_ref[src_ref[t]] += prod
+    for t in range(tiles_ref.shape[0]):
+        prod = jnp.dot(
+            every_ref[slot(dest_ref[t], block_ref[t], nblk, stride)], tiles_ref[t], preferred_element_type=F32
+        )
+        acc_ref[src_ref[t]] += prod
     for b in range(nblk):
         out_ref[:, b * BLK : (b + 1) * BLK] = acc_ref[b].astype(BF)
 
@@ -123,7 +135,7 @@
     rows = nblk * BLK
     for r in range(cores * chips):
         for b in range(nblk):
-            all_ref[r * panel : (r + 1) * panel, b * BLK : (b + 1) * BLK] = got_ref[r % cores, r // cores, b]
+            all_ref[r * panel : (r + 1) * panel, b * BLK : (b + 1) * BLK] = got_ref[r % cores, [m[0] for m in X_ORDER].index(r // cores), b]
     own = pl.ds(pl.multiple_of(rep_ref[0] * panel, panel), panel)
     weight = both_ref[:, rows:]
     mixed = jnp.dot(weight, all_ref[...], preferred_element_type=F32)
@@ -173,11 +185,9 @@
     stride = NZ8 * nblk + halves
     rep = lax.axis_index(("x", "core")).astype(jnp.int32).reshape(1)
     shape = jax.ShapeDtypeStruct
-    tile_scratch = [pltpu.VMEM((tiles, BLK, BLK), BF), pltpu.SemaphoreType.DMA((CHUNKS,))]
     tile_bytes = tiles * BLK * BLK * 2
     tile_flops = 2 * tiles * panel * BLK * BLK
     places = tuple(map(in_hbm, (tile_dest[:, 0], tile_block, tile_source)))
-    tile_values = in_hbm(tile_values)
 
     parts = call(
         scatter_products,
@@ -187,23 +197,24 @@
         [
             pltpu.VMEM((ntot, panel, BLK), F32),
             pltpu.VMEM((ntot, panel, BLK), BF),
-            *tile_scratch,
-            pltpu.SemaphoreType.DMA((CHUNKS,)),
+            pltpu.VMEM((tiles, BLK, BLK), BF),
+            pltpu.SemaphoreType.DMA((len(CHUNKS),)),
+            pltpu.SemaphoreType.DMA((WRITES,)),
         ],
         flops=tile_flops,
         nbytes=tile_bytes,
         outs=HBM,
-    )(*places, in_hbm(feats), tile_values)
-
-    got = lax.all_to_all(parts.reshape(near, NZ8 * nblk, panel, BLK), ("y", "zp"), 0, 0)
+    )(*places, in_hbm(feats), in_hbm(tile_values))
+
+    got = exchange(parts.reshape(near, NZ8 * nblk, panel, BLK), ("y", "zp"), NEAR_ORDER)
     both = lax.all_gather(
         jnp.concatenate([cotangent, weight.T], axis=1), ("x", "core"), axis=0, tiled=True
     )
     got, both = lax.optimization_barrier((got, both))
     half = call(sum_first, "sum_near", shape((NZ8 * nblk, panel, BLK), BF), [VMEM], nbytes=ntot * panel * BLK * 2)(got)
-    got = lax.all_to_all(half.reshape(NZ8, nblk, panel, BLK), "z8", 0, 0)
+    got = exchange(half.reshape(NZ8, nblk, panel, BLK), ("z8",), FAR_ORDER)
     mine = call(finish_sum, "sum_far", shape((NX, nblk, panel, BLK), BF), [VMEM], nbytes=1 << 19)(got)
-    gathered = lax.all_gather(lax.all_to_all(mine, "x", 0, 0), "core", axis=0)
+    gathered = lax.all_gather(exchange(mine, ("x",), X_ORDER), "core", axis=0)
 
     hidden, sent = call(
         middle,
@@ -218,7 +229,7 @@
         nbytes=1 << 20,
     )(rep, gathered, both)
 
-    col = lax.all_to_all(sent, "z8", 0, 0)
+    col = exchange(sent, ("z8",), FAR_ORDER)
     copies = call(
         spread,
         "spread",
@@ -228,14 +239,14 @@
         nbytes=ntot * panel * BLK * 2,
         outs=HBM,
     )(col)
-    every = lax.all_to_all(copies, ("y", "zp"), 0, 0)
+    every = exchange(copies, ("y", "zp"), NEAR_ORDER)
 
     input_grad, weight_grad = call(
         gather_products,
         "gather_products",
         (shape((panel, rows), BF), shape((panel, full), F32)),
-        [SMEM, SMEM, SMEM, VMEM, HBM],
-        [pltpu.VMEM((nblk, panel, BLK), F32), *tile_scratch],
+        [SMEM, SMEM, SMEM, VMEM, VMEM],
+        [pltpu.VMEM((nblk, panel, BLK), F32)],
         flops=tile_flops,
         nbytes=tile_bytes,
     )(*places, every.reshape(near * stride, panel, BLK), tile_values)

time: 157 us -> 150 us (0.955)
  the two profiles are of different devices: /device:TPU:1 before, /device:TPU:2 now
where the time goes in v4:
time: 150 us
  blocking collectives  110 us (73%)
  waiting for transfers between devices  16.6 us (11%)
  Pallas kernels  11.9 us (8%)
  starting transfers between devices  10.7 us (7%)
    all_to_all x3, blocking collectives, exchange(): lax.all_to_all(flat, AXES, 0, 0, tiled=True, axis_index_groups=groups)  94.4 us
    all_to_all x2, waiting for transfers between devices, exchange(): lax.all_to_all(flat, AXES, 0, 0, tiled=True, axis_index_groups=groups)  16.6 us
    all_gather x1, blocking collectives, per_device(): lax.all_gather(jnp.concatenate([cotangent, weight.T], axis=1), ('x', 'cor...  13.5 us
    all_to_all x2, starting transfers between devices, exchange(): lax.all_to_all(flat, AXES, 0, 0, tiled=True, axis_index_groups=groups)  10.7 us
    pallas_call x1, Pallas kernels, per_device(): call(scatter_products, 'scatter_products', pltpu.HBM((ntot, panel, BLK),...  5.96 us
  transfers between devices with their start and end apart: 2, of which 2 were waited for; matrix products, arithmetic and copies ran while one was open for 0% of the time, Pallas kernels for 0%

profile of v4, /device:TPU:2, one launch (start us, length us, event | category | flops | bytes accessed | tf_op | source)
XLA Modules:
  0.0 149.9 jit_solution(11107487791424240605)
XLA Ops:
  0.6 6.0 %scatter_products.1 = bf16[256,32,128]{2,1,0:T(8,128)(2,1)} custom-call(s32[128]{0:T(128)} %bitcast.24, s32[128]{0:T(128)} %block_ref.3, s32[128]{0:T(128)} %src_ref.3, bf16[32,512]{1,0:T(8,128)(2,1)} %feats_ref.1, bf16[128,128,128]{2,1,0:T(8,128)(2,1)} %tiles_ref.3), custom_call_target="tpu_custom_call" | custom-call | flops 134217728 | bytes 4194304 | tf_op jit(solution)/shard_map/scatter_products/pallas_call | solution.py:192
  6.6 0.0 copy-start.1
  6.6 0.0 copy-start.2
  6.6 5.8 %all-to-all-start = ((bf16[8,1024,128]{2,1,0:T(8,128)(2,1)}), bf16[8,1024,128]{2,1,0:T(8,128)(2,1)S(1)}, u32[]{:S(2)}, u32[]{:S(2)}) async-start(bf16[8,1024,128]{2,1,0:T(8,128)(2,1)} %bitcast.21), calls=%async_computation | async-start | bytes 4194304 | tf_op jit(solution)/shard_map/all_to_all | solution.py:42
  12.5 0.0 copy-done.1
  12.5 0.0 copy-done.2
  12.5 13.5 %all_gather.6.both_ref = bf16[256,768]{1,0:T(8,128)(2,1)S(1)} all-gather(bf16[32,768]{1,0:T(8,128)(2,1)S(1)} %pad_maximum_fusion), channel_id=1, replica_groups=mesh['y'=4,'z8'=8,'zp'=2,'x'=4,'core'=2] {'x','core'}, dimensions={0}, use_global_device_ids=true | all-gather | bytes 442368 | tf_op jit(solution)/shard_map/all_gather | solution.py:210
  26.0 12.5 %all-to-all-done = bf16[8,1024,128]{2,1,0:T(8,128)(2,1)S(1)} async-done(((bf16[8,1024,128]{2,1,0:T(8,128)(2,1)}), bf16[8,1024,128]{2,1,0:T(8,128)(2,1)S(1)}, u32[]{:S(2)}, u32[]{:S(2)}) %all-to-all-start) | async-done | bytes 2097184 | tf_op jit(solution)/shard_map/all_to_all | solution.py:42
  38.5 0.3 sum_near.1
  38.8 28.0 %all_to_all.25 = bf16[8,128,128]{2,1,0:T(8,128)(2,1)S(1)} all-to-all(bf16[8,128,128]{2,1,0:T(8,128)(2,1)S(1)} %bitcast.17), channel_id=1, replica_groups={{0,64,32,96,16,80,48,112},{1,65,33,97,17,81,49,113},{2,66,34,98,18,82,5..., dimensions={0} | all-to-all | bytes 524288 | tf_op jit(solution)/shard_map/all_to_all | solution.py:42
  66.8 0.7 sum_far.1
  67.5 4.8 %all-to-all-start.2 = ((bf16[4,128,128]{2,1,0:T(8,128)(2,1)}), bf16[4,128,128]{2,1,0:T(8,128)(2,1)S(1)}, u32[]{:S(2)}, u32[]{:S(2)}) async-start(bf16[4,128,128]{2,1,0:T(8,128)(2,1)} %bitcast.7), calls=%async_computation.2 | async-start | bytes 262144 | tf_op jit(solution)/shard_map/all_to_all | solution.py:42
  72.3 4.2 %all-to-all-done.2 = bf16[4,128,128]{2,1,0:T(8,128)(2,1)S(1)} async-done(((bf16[4,128,128]{2,1,0:T(8,128)(2,1)}), bf16[4,128,128]{2,1,0:T(8,128)(2,1)S(1)}, u32[]{:S(2)}, u32[]{:S(2)}) %all-to-all-start.2) | async-done | bytes 131104 | tf_op jit(solution)/shard_map/all_to_all | solution.py:42
  76.5 2.0 %all_gather.7.got_ref = bf16[2,4,4,32,128]{4,3,2,1,0:T(8,128)(2,1)S(1)} all-gather(bf16[1,4,4,32,128]{4,3,2,1,0:T(8,128)(2,1)S(1)} %bitcast.22), channel_id=1, replica_groups=mesh['y'=4,'z8'=8,'zp'=2,'x'=4,'core'=2] {'core'}, dimensions={0}, use_global_device_ids=true | all-gather | bytes 393216 | tf_op jit(solution)/shard_map/all_gather | solution.py:217
  78.5 1.0 middle.1
  79.4 30.7 %all_to_all.26 = bf16[8,192,128]{2,1,0:T(8,128)(2,1)S(1)} all-to-all(bf16[8,192,128]{2,1,0:T(8,128)(2,1)S(1)} %bitcast.19), channel_id=1, replica_groups={{0,64,32,96,16,80,48,112},{1,65,33,97,17,81,49,113},{2,66,34,98,18,82,5..., dimensions={0} | all-to-all | bytes 786432 | tf_op jit(solution)/shard_map/all_to_all | solution.py:42
  110.1 1.5 spread.1
  111.6 0.0 copy-start
  111.6 35.7 %all_to_all.27 = bf16[8,1088,128]{2,1,0:T(8,128)(2,1)S(1)} all-to-all(bf16[8,1088,128]{2,1,0:T(8,128)(2,1)} %bitcast.20), channel_id=1, replica_groups={{0,128,256,384,8,136,264,392},{1,129,257,385,9,137,265,393},{2,130,258,..., dimensions={0} | all-to-all | bytes 4456448 | tf_op jit(solution)/shard_map/all_to_all | solution.py:42
  147.4 0.0 copy-done
  147.4 2.6 %gather_products.1 = (bf16[32,512]{1,0:T(8,128)(2,1)}, f32[32,256]{1,0:T(8,128)}) custom-call(s32[128]{0:T(128)} %bitcast.25, s32[128]{0:T(128)} %block_ref.3, s32[128]{0:T(128)} %src_ref.3, bf16[272,32,128]{2,1,0:T(8,128)(2,1)S(1)} %bitcast.14, bf16[128,128,128]{2,1,0:T(8,128)(2,1)S(1)} %copy-done), custom_call_target="tpu_custom_call" | custom-call | flops 134217728 | bytes 4194304 | tf_op jit(solution)/shard_map/gather_products/pallas_call | solution.py:244
  (1 shorter events, 0.0 us)
Async XLA Ops:
  6.6 5.9 %copy-start.1 = (bf16[32,512]{1,0:T(8,128)(2,1)S(1)}, bf16[32,512]{1,0:T(8,128)(2,1)}, u32[]{:S(2)}) copy-start(bf16[32,512]{1,0:T(8,128)(2,1)} %param.13) | copy-start | bytes 98308
  6.6 5.9 %copy-start.2 = (bf16[256,32]{0,1:T(8,128)(2,1)S(1)}, bf16[256,32]{0,1:T(8,128)(2,1)}, u32[]{:S(2)}) copy-start(bf16[256,32]{0,1:T(8,128)(2,1)} %param.8) | copy-start | bytes 49156
  6.6 31.9 %all-to-all-start = ((bf16[8,1024,128]{2,1,0:T(8,128)(2,1)}), bf16[8,1024,128]{2,1,0:T(8,128)(2,1)S(1)}, u32[]{:S(2)}, u32[]{:S(2)}) async-start(bf16[8,1024,128]{2,1,0:T(8,128)(2,1)} %bitcast.21), calls=%async_computation | async-start | bytes 4194304 | tf_op jit(solution)/shard_map/all_to_all | solution.py:42
  67.5 9.0 %all-to-all-start.2 = ((bf16[4,128,128]{2,1,0:T(8,128)(2,1)}), bf16[4,128,128]{2,1,0:T(8,128)(2,1)S(1)}, u32[]{:S(2)}, u32[]{:S(2)}) async-start(bf16[4,128,128]{2,1,0:T(8,128)(2,1)} %bitcast.7), calls=%async_computation.2 | async-start | bytes 262144 | tf_op jit(solution)/shard_map/all_to_all | solution.py:42
  111.6 35.7 %copy-start = (bf16[128,128,128]{2,1,0:T(8,128)(2,1)S(1)}, bf16[128,128,128]{2,1,0:T(8,128)(2,1)}, u32[]{:S(2)}) copy-start(bf16[128,128,128]{2,1,0:T(8,128)(2,1)} %tiles_ref.3) | copy-start | bytes 12582916

commit v5 on v4

--- a/solution.py
+++ b/solution.py
@@ -29,23 +29,24 @@
 SIZES = (NY, NZ8, NP, NX, NC)
 NEAR_ORDER = [(0, 0), (1, 0), (2, 0), (3, 0), (0, 1), (1, 1), (2, 1), (3, 1)]
 FAR_ORDER = [(0,), (4,), (2,), (6,), (1,), (5,), (3,), (7,)]
+NEAR_TURN, FAR_TURN = 4, 7
 X_ORDER = [(0,), (2,), (1,), (3,)]
 
 
-def exchange(x, axes, order):
+def exchange(x, axes, order, turn=0):
     others = [a for a in AXES if a not in axes]
     ranks = np.arange(math.prod(SIZES)).reshape(SIZES)
     ranks = ranks.transpose([AXES.index(a) for a in (*others, *axes)])
     ranks = ranks.reshape(-1, *(SIZES[AXES.index(a)] for a in axes))
-    groups = [[int(r[m]) for m in order] for r in ranks]
+    groups = [[int(r[order[i ^ (turn * (r.flat[0] % NC))]]) for i in range(len(order))] for r in ranks]
     flat = x.reshape(x.shape[0], -1, BLK)
     return lax.all_to_all(flat, AXES, 0, 0, tiled=True, axis_index_groups=groups).reshape(x.shape)
 
 
-def slot(dest, block, nblk, stride):
+def slot(dest, block, core, nblk, stride):
     y, z = lax.shift_right_logical(dest, 4), dest & 15
-    near = (z & 1) * 4 + y
-    far = (z & 2) * 2 + lax.shift_right_logical(z & 4, 1) + lax.shift_right_logical(z, 3)
+    near = ((z & 1) * 4 + y) ^ (core * NEAR_TURN)
+    far = ((z & 2) * 2 + lax.shift_right_logical(z & 4, 1) + lax.shift_right_logical(z, 3)) ^ (core * FAR_TURN)
     return near * stride + far * nblk + block
 
 
@@ -64,7 +65,7 @@
 
 
 def scatter_products(
-    dest_ref, block_ref, src_ref, feats_ref, tiles_ref, out_ref, acc_ref, half_ref, buf_ref, sems, out_sems
+    core_ref, dest_ref, block_ref, src_ref, feats_ref, tiles_ref, out_ref, acc_ref, half_ref, buf_ref, sems, out_sems
 ):
     copies = []
     for c, n in enumerate(CHUNKS):
@@ -83,7 +84,7 @@
                 (((1,), (1,)), ((), ())),
                 preferred_element_type=F32,
             )
-            acc_ref[slot(dest_ref[t], block_ref[t], nblk, NZ8 * nblk)] += prod
+            acc_ref[slot(dest_ref[t], block_ref[t], core_ref[0], nblk, NZ8 * nblk)] += prod
     m = out_ref.shape[0] // WRITES
     writes = []
     for c in range(WRITES):
@@ -95,7 +96,7 @@
         writes[c].wait()
 
 
-def gather_products(dest_ref, block_ref, src_ref, every_ref, tiles_ref, out_ref, wg_ref, acc_ref):
+def gather_products(core_ref, dest_ref, block_ref, src_ref, every_ref, tiles_ref, out_ref, wg_ref, acc_ref):
     acc_ref[...] = jnp.zeros_like(acc_ref)
     nblk, panel, _ = acc_ref.shape
     stride = every_ref.shape[0] // (NY * NP)
@@ -106,7 +107,7 @@
         wg_ref[:, h * BLK : (h + 1) * BLK] = total * float(nblk * BLK * NY * NZ) ** (-0.5)
     for t in range(tiles_ref.shape[0]):
         prod = jnp.dot(
-            every_ref[slot(dest_ref[t], block_ref[t], nblk, stride)], tiles_ref[t], preferred_element_type=F32
+            every_ref[slot(dest_ref[t], block_ref[t], core_ref[0], nblk, stride)], tiles_ref[t], preferred_element_type=F32
         )
         acc_ref[src_ref[t]] += prod
     for b in range(nblk):
@@ -157,21 +158,20 @@
             msg_ref[z, nblk + h] = wgrad[:, h * BLK : (h + 1) * BLK]
 
 
-def spread(got_ref, msg_ref, one_ref, sems):
+def spread(got_ref, msg_ref):
     pairs, blocks, panel, _ = got_ref.shape
-    nblk = (one_ref.shape[0] - blocks) // (pairs - 1)
-    for z in range(pairs):
-        one_ref[z * nblk : (z + 1) * nblk] = got_ref[z, :nblk]
+    near, stride = msg_ref.shape[:2]
+    nblk = (stride - blocks) // (pairs - 1)
     for h in range(blocks - nblk):
         total = jnp.zeros((panel, BLK), F32)
         for z in range(pairs):
             total += got_ref[z, nblk + h].astype(F32)
-        one_ref[pairs * nblk + h] = total.astype(BF)
-    copies = [pltpu.make_async_copy(one_ref, msg_ref.at[k], sems.at[k]) for k in range(msg_ref.shape[0])]
-    for c in copies:
-        c.start()
-    for c in copies:
-        c.wait()
+        for k in range(near):
+            msg_ref[k, pairs * nblk + h] = total.astype(BF)
+    for z in range(pairs):
+        one = got_ref[z, :nblk]
+        for k in range(near):
+            msg_ref[k, z * nblk : (z + 1) * nblk] = one
 
 
 def per_device(feats, weight, tile_values, tile_dest, tile_block, tile_source, cotangent):
@@ -187,13 +187,14 @@
     shape = jax.ShapeDtypeStruct
     tile_bytes = tiles * BLK * BLK * 2
     tile_flops = 2 * tiles * panel * BLK * BLK
-    places = tuple(map(in_hbm, (tile_dest[:, 0], tile_block, tile_source)))
+    core = lax.axis_index("core").astype(jnp.int32).reshape(1)
+    places = (core, *map(in_hbm, (tile_dest[:, 0], tile_block, tile_source)))
 
     parts = call(
         scatter_products,
         "scatter_products",
         pltpu.HBM((ntot, panel, BLK), BF),
-        [SMEM, SMEM, SMEM, VMEM, HBM],
+        [SMEM, SMEM, SMEM, SMEM, VMEM, HBM],
         [
             pltpu.VMEM((ntot, panel, BLK), F32),
             pltpu.VMEM((ntot, panel, BLK), BF),
@@ -206,13 +207,13 @@
         outs=HBM,
     )(*places, in_hbm(feats), in_hbm(tile_values))
 
-    got = exchange(parts.reshape(near, NZ8 * nblk, panel, BLK), ("y", "zp"), NEAR_ORDER)
+    got = exchange(parts.reshape(near, NZ8 * nblk, panel, BLK), ("y", "zp"), NEAR_ORDER, NEAR_TURN)
     both = lax.all_gather(
         jnp.concatenate([cotangent, weight.T], axis=1), ("x", "core"), axis=0, tiled=True
     )
     got, both = lax.optimization_barrier((got, both))
     half = call(sum_first, "sum_near", shape((NZ8 * nblk, panel, BLK), BF), [VMEM], nbytes=ntot * panel * BLK * 2)(got)
-    got = exchange(half.reshape(NZ8, nblk, panel, BLK), ("z8",), FAR_ORDER)
+    got = exchange(half.reshape(NZ8, nblk, panel, BLK), ("z8",), FAR_ORDER, FAR_TURN)
     mine = call(finish_sum, "sum_far", shape((NX, nblk, panel, BLK), BF), [VMEM], nbytes=1 << 19)(got)
     gathered = lax.all_gather(exchange(mine, ("x",), X_ORDER), "core", axis=0)
 
@@ -229,23 +230,21 @@
         nbytes=1 << 20,
     )(rep, gathered, both)
 
-    col = exchange(sent, ("z8",), FAR_ORDER)
+    col = exchange(sent, ("z8",), FAR_ORDER, FAR_TURN)
     copies = call(
         spread,
         "spread",
-        pltpu.HBM((near, stride, panel, BLK), BF),
+        shape((near, stride, panel, BLK), BF),
         [VMEM],
-        [pltpu.VMEM((stride, panel, BLK), BF), pltpu.SemaphoreType.DMA((near,))],
         nbytes=ntot * panel * BLK * 2,
-        outs=HBM,
     )(col)
-    every = exchange(copies, ("y", "zp"), NEAR_ORDER)
+    every = exchange(copies, ("y", "zp"), NEAR_ORDER, NEAR_TURN)
 
     input_grad, weight_grad = call(
         gather_products,
         "gather_products",
         (shape((panel, rows), BF), shape((panel, full), F32)),
-        [SMEM, SMEM, SMEM, VMEM, VMEM],
+        [SMEM, SMEM, SMEM, SMEM, VMEM, VMEM],
         [pltpu.VMEM((nblk, panel, BLK), F32)],
         flops=tile_flops,
         nbytes=tile_bytes,

time: 150 us -> 148 us (0.987)
  the two profiles are of different devices: /device:TPU:2 before, /device:TPU:32 now
where the time goes in v5:
time: 148 us; the launch traced here: 147 us
  blocking collectives  108 us (73%)
  waiting for transfers between devices  14.4 us (10%)
  starting transfers between devices  13.3 us (9%)
  Pallas kernels  10.8 us (7%)
    all_to_all x3, blocking collectives, exchange(): lax.all_to_all(flat, AXES, 0, 0, tiled=True, axis_index_groups=groups)  93.1 us
    all_to_all x2, waiting for transfers between devices, exchange(): lax.all_to_all(flat, AXES, 0, 0, tiled=True, axis_index_groups=groups)  14.4 us
    all_to_all x2, starting transfers between devices, exchange(): lax.all_to_all(flat, AXES, 0, 0, tiled=True, axis_index_groups=groups)  13.3 us
    all_gather x1, blocking collectives, per_device(): lax.all_gather(jnp.concatenate([cotangent, weight.T], axis=1), ('x', 'cor...  13 us
    pallas_call x1, Pallas kernels, per_device(): call(scatter_products, 'scatter_products', pltpu.HBM((ntot, panel, BLK),...  5.96 us
  transfers between devices with their start and end apart: 2, of which 2 were waited for; matrix products, arithmetic and copies ran while one was open for 0% of the time, Pallas kernels for 0%

profile of v5, /device:TPU:32, one launch (start us, length us, event | category | flops | bytes accessed | tf_op | source)
XLA Modules:
  0.0 147.4 jit_solution(2114339868370882346)
XLA Ops:
  0.6 6.0 %scatter_products.1 = bf16[256,32,128]{2,1,0:T(8,128)(2,1)} custom-call(s32[1]{0:T(128)} %bitcast.1.core_ref, s32[128]{0:T(128)} %bitcast.25, s32[128]{0:T(128)} %block_ref.3, s32[128]{0:T(128)} %src_ref.3, bf16[32,512]{1,0:T(8,128)(2,1)} %feats_ref.1, bf16[128,128,128]{2,1,0:T(8,128)(2,1)} %tiles_ref.3), custom_call_target="tpu_custom_call" | custom-call | flops 134217728 | bytes 4194304 | tf_op jit(solution)/shard_map/scatter_products/pallas_call | solution.py:193
  6.6 0.0 copy-start.1
  6.6 0.0 copy-start.2
  6.6 9.0 %all-to-all-start = ((bf16[8,1024,128]{2,1,0:T(8,128)(2,1)}), bf16[8,1024,128]{2,1,0:T(8,128)(2,1)S(1)}, u32[]{:S(2)}, u32[]{:S(2)}) async-start(bf16[8,1024,128]{2,1,0:T(8,128)(2,1)} %bitcast.22), calls=%async_computation | async-start | bytes 4194304 | tf_op jit(solution)/shard_map/all_to_all | solution.py:43
  15.6 0.0 copy-done.1
  15.7 0.0 copy-done.2
  15.7 13.0 %all_gather.6.both_ref = bf16[256,768]{1,0:T(8,128)(2,1)S(1)} all-gather(bf16[32,768]{1,0:T(8,128)(2,1)S(1)} %pad_maximum_fusion), channel_id=1, replica_groups=mesh['y'=4,'z8'=8,'zp'=2,'x'=4,'core'=2] {'x','core'}, dimensions={0}, use_global_device_ids=true | all-gather | bytes 442368 | tf_op jit(solution)/shard_map/all_gather | solution.py:211
  28.6 8.5 %all-to-all-done = bf16[8,1024,128]{2,1,0:T(8,128)(2,1)S(1)} async-done(((bf16[8,1024,128]{2,1,0:T(8,128)(2,1)}), bf16[8,1024,128]{2,1,0:T(8,128)(2,1)S(1)}, u32[]{:S(2)}, u32[]{:S(2)}) %all-to-all-start) | async-done | bytes 2097184 | tf_op jit(solution)/shard_map/all_to_all | solution.py:43
  37.1 0.3 sum_near.1
  37.4 29.3 %all_to_all.25 = bf16[8,128,128]{2,1,0:T(8,128)(2,1)S(1)} all-to-all(bf16[8,128,128]{2,1,0:T(8,128)(2,1)S(1)} %bitcast.19), channel_id=1, replica_groups={{0,64,32,96,16,80,48,112},{113,49,81,17,97,33,65,1},{2,66,34,98,18,82,5..., dimensions={0} | all-to-all | bytes 524288 | tf_op jit(solution)/shard_map/all_to_all | solution.py:43
  66.7 0.7 sum_far.1
  67.4 4.3 %all-to-all-start.2 = ((bf16[4,128,128]{2,1,0:T(8,128)(2,1)}), bf16[4,128,128]{2,1,0:T(8,128)(2,1)S(1)}, u32[]{:S(2)}, u32[]{:S(2)}) async-start(bf16[4,128,128]{2,1,0:T(8,128)(2,1)} %bitcast.8), calls=%async_computation.2 | async-start | bytes 262144 | tf_op jit(solution)/shard_map/all_to_all | solution.py:43
  71.7 5.9 %all-to-all-done.2 = bf16[4,128,128]{2,1,0:T(8,128)(2,1)S(1)} async-done(((bf16[4,128,128]{2,1,0:T(8,128)(2,1)}), bf16[4,128,128]{2,1,0:T(8,128)(2,1)S(1)}, u32[]{:S(2)}, u32[]{:S(2)}) %all-to-all-start.2) | async-done | bytes 131104 | tf_op jit(solution)/shard_map/all_to_all | solution.py:43
  77.6 2.0 %all_gather.7.got_ref = bf16[2,4,4,32,128]{4,3,2,1,0:T(8,128)(2,1)S(1)} all-gather(bf16[1,4,4,32,128]{4,3,2,1,0:T(8,128)(2,1)S(1)} %bitcast.23), channel_id=1, replica_groups=mesh['y'=4,'z8'=8,'zp'=2,'x'=4,'core'=2] {'core'}, dimensions={0}, use_global_device_ids=true | all-gather | bytes 393216 | tf_op jit(solution)/shard_map/all_gather | solution.py:218
  79.6 1.0 middle.1
  80.6 31.9 %all_to_all.26 = bf16[8,192,128]{2,1,0:T(8,128)(2,1)S(1)} all-to-all(bf16[8,192,128]{2,1,0:T(8,128)(2,1)S(1)} %bitcast.21), channel_id=1, replica_groups={{0,64,32,96,16,80,48,112},{113,49,81,17,97,33,65,1},{2,66,34,98,18,82,5..., dimensions={0} | all-to-all | bytes 786432 | tf_op jit(solution)/shard_map/all_to_all | solution.py:43
  112.5 0.3 spread.1
  112.9 0.0 copy-start
  112.9 31.9 %all_to_all.27 = bf16[8,1088,128]{2,1,0:T(8,128)(2,1)S(1)} all-to-all(bf16[8,1088,128]{2,1,0:T(8,128)(2,1)S(1)} %bitcast.16), channel_id=1, replica_groups={{0,128,256,384,8,136,264,392},{9,137,265,393,1,129,257,385},{2,130,258,..., dimensions={0} | all-to-all | bytes 4456448 | tf_op jit(solution)/shard_map/all_to_all | solution.py:43
  144.8 0.0 copy-done
  144.8 2.6 %gather_products.1 = (bf16[32,512]{1,0:T(8,128)(2,1)}, f32[32,256]{1,0:T(8,128)}) custom-call(s32[1]{0:T(128)} %bitcast.1.core_ref, s32[128]{0:T(128)} %bitcast.26, s32[128]{0:T(128)} %block_ref.3, s32[128]{0:T(128)} %src_ref.3, bf16[272,32,128]{2,1,0:T(8,128)(2,1)S(1)} %bitcast.15, bf16[128,128,128]{2,1,0:T(8,128)(2,1)S(1)} %copy-done), custom_call_target="tpu_custom_call" | custom-call | flops 134217728 | bytes 4194304 | tf_op jit(solution)/shard_map/gather_products/pallas_call | solution.py:243
  (1 shorter events, 0.0 us)
Async XLA Ops:
  6.6 9.0 %copy-start.1 = (bf16[32,512]{1,0:T(8,128)(2,1)S(1)}, bf16[32,512]{1,0:T(8,128)(2,1)}, u32[]{:S(2)}) copy-start(bf16[32,512]{1,0:T(8,128)(2,1)} %param.13) | copy-start | bytes 98308
  6.6 9.0 %copy-start.2 = (bf16[256,32]{0,1:T(8,128)(2,1)S(1)}, bf16[256,32]{0,1:T(8,128)(2,1)}, u32[]{:S(2)}) copy-start(bf16[256,32]{0,1:T(8,128)(2,1)} %param.8) | copy-start | bytes 49156
  6.6 30.5 %all-to-all-start = ((bf16[8,1024,128]{2,1,0:T(8,128)(2,1)}), bf16[8,1024,128]{2,1,0:T(8,128)(2,1)S(1)}, u32[]{:S(2)}, u32[]{:S(2)}) async-start(bf16[8,1024,128]{2,1,0:T(8,128)(2,1)} %bitcast.22), calls=%async_computation | async-start | bytes 4194304 | tf_op jit(solution)/shard_map/all_to_all | solution.py:43
  67.4 10.2 %all-to-all-start.2 = ((bf16[4,128,128]{2,1,0:T(8,128)(2,1)}), bf16[4,128,128]{2,1,0:T(8,128)(2,1)S(1)}, u32[]{:S(2)}, u32[]{:S(2)}) async-start(bf16[4,128,128]{2,1,0:T(8,128)(2,1)} %bitcast.8), calls=%async_computation.2 | async-start | bytes 262144 | tf_op jit(solution)/shard_map/all_to_all | solution.py:43
  112.9 31.9 %copy-start = (bf16[128,128,128]{2,1,0:T(8,128)(2,1)S(1)}, bf16[128,128,128]{2,1,0:T(8,128)(2,1)}, u32[]{:S(2)}) copy-start(bf16[128,128,128]{2,1,0:T(8,128)(2,1)} %tiles_ref.3) | copy-start | bytes 12582916

commit v6 on v5

--- a/solution.py
+++ b/solution.py
@@ -65,7 +65,7 @@
 
 
 def scatter_products(
-    core_ref, dest_ref, block_ref, src_ref, feats_ref, tiles_ref, out_ref, acc_ref, half_ref, buf_ref, sems, out_sems
+    rep_ref, dest_ref, block_ref, src_ref, feats_ref, tiles_ref, out_ref, acc_ref, half_ref, buf_ref, sems, out_sems
 ):
     copies = []
     for c, n in enumerate(CHUNKS):
@@ -84,7 +84,7 @@
                 (((1,), (1,)), ((), ())),
                 preferred_element_type=F32,
             )
-            acc_ref[slot(dest_ref[t], block_ref[t], core_ref[0], nblk, NZ8 * nblk)] += prod
+            acc_ref[slot(dest_ref[t], block_ref[t], rep_ref[0] & 1, nblk, NZ8 * nblk)] += prod
     m = out_ref.shape[0] // WRITES
     writes = []
     for c in range(WRITES):
@@ -96,7 +96,7 @@
         writes[c].wait()
 
 
-def gather_products(core_ref, dest_ref, block_ref, src_ref, every_ref, tiles_ref, out_ref, wg_ref, acc_ref):
+def gather_products(rep_ref, dest_ref, block_ref, src_ref, every_ref, tiles_ref, out_ref, wg_ref, acc_ref):
     acc_ref[...] = jnp.zeros_like(acc_ref)
     nblk, panel, _ = acc_ref.shape
     stride = every_ref.shape[0] // (NY * NP)
@@ -107,7 +107,7 @@
         wg_ref[:, h * BLK : (h + 1) * BLK] = total * float(nblk * BLK * NY * NZ) ** (-0.5)
     for t in range(tiles_ref.shape[0]):
         prod = jnp.dot(
-            every_ref[slot(dest_ref[t], block_ref[t], core_ref[0], nblk, stride)], tiles_ref[t], preferred_element_type=F32
+            every_ref[slot(dest_ref[t], block_ref[t], rep_ref[0] & 1, nblk, stride)], tiles_ref[t], preferred_element_type=F32
         )
         acc_ref[src_ref[t]] += prod
     for b in range(nblk):
@@ -183,12 +183,11 @@
     full = NX * NC * panel
     halves = full // BLK
     stride = NZ8 * nblk + halves
-    rep = lax.axis_index(("x", "core")).astype(jnp.int32).reshape(1)
     shape = jax.ShapeDtypeStruct
     tile_bytes = tiles * BLK * BLK * 2
     tile_flops = 2 * tiles * panel * BLK * BLK
-    core = lax.axis_index("core").astype(jnp.int32).reshape(1)
-    places = (core, *map(in_hbm, (tile_dest[:, 0], tile_block, tile_source)))
+    rep = lax.axis_index(("x", "core")).astype(jnp.int32).reshape(1)
+    places = (rep, *map(in_hbm, (tile_dest[:, 0], tile_block, tile_source)))
 
     parts = call(
         scatter_products,

time: 148 us -> 147 us (level)
  blocking collectives: 108 us -> 118 us
  waiting for transfers between devices: 14.4 us -> 8.5 us
  starting transfers between devices: 13.3 us -> 9.02 us
    all_to_all x3 -> x4, blocking collectives: 93.1 us -> 103 us  [exchange(): lax.all_to_all(flat, AXES, 0, 0, tiled=True, axis_index_groups=groups)]
    all_to_all x2 -> x1, waiting for transfers between devices: 14.4 us -> 8.5 us  [exchange(): lax.all_to_all(flat, AXES, 0, 0, tiled=True, axis_index_groups=groups)]
    all_to_all x2 -> x1, starting transfers between devices: 13.3 us -> 9.02 us  [exchange(): lax.all_to_all(flat, AXES, 0, 0, tiled=True, axis_index_groups=groups)]
  transfers between devices with their start and end apart: 2 -> 1, of which waited for: 2 -> 1; matrix products, arithmetic and copies ran while one was open for 0% -> 0% of each run, Pallas kernels for 0% -> 0%
where the time goes in v6:
time: 147 us
  blocking collectives  118 us (80%)
  Pallas kernels  10.2 us (7%)
  starting transfers between devices  9.02 us (6%)
  waiting for transfers between devices  8.5 us (6%)
    all_to_all x4, blocking collectives, exchange(): lax.all_to_all(flat, AXES, 0, 0, tiled=True, axis_index_groups=groups)  103 us
    all_gather x1, blocking collectives, per_device(): lax.all_gather(jnp.concatenate([cotangent, weight.T], axis=1), ('x', 'cor...  13 us
    all_to_all x1, starting transfers between devices, exchange(): lax.all_to_all(flat, AXES, 0, 0, tiled=True, axis_index_groups=groups)  9.02 us
    all_to_all x1, waiting for transfers between devices, exchange(): lax.all_to_all(flat, AXES, 0, 0, tiled=True, axis_index_groups=groups)  8.5 us
    pallas_call x1, Pallas kernels, per_device(): call(scatter_products, 'scatter_products', pltpu.HBM((ntot, panel, BLK),...  5.97 us
  transfers between devices with their start and end apart: 1, of which 1 were waited for; matrix products, arithmetic and copies ran while one was open for 0% of the time, Pallas kernels for 0%

profile of v6, /device:TPU:32, one launch (start us, length us, event | category | flops | bytes accessed | tf_op | source)
XLA Modules:
  0.0 146.6 jit_solution(13774217272249093242)
XLA Ops:
  0.6 6.0 %scatter_products.1 = bf16[256,32,128]{2,1,0:T(8,128)(2,1)} custom-call(s32[1]{0:T(128)} %bitcast.rep_ref, s32[128]{0:T(128)} %bitcast.25, s32[128]{0:T(128)} %block_ref.3, s32[128]{0:T(128)} %src_ref.3, bf16[32,512]{1,0:T(8,128)(2,1)} %feats_ref.1, bf16[128,128,128]{2,1,0:T(8,128)(2,1)} %tiles_ref.3), custom_call_target="tpu_custom_call" | custom-call | flops 134217728 | bytes 4194304 | tf_op jit(solution)/shard_map/scatter_products/pallas_call | solution.py:192
  6.6 0.0 copy-start.1
  6.6 0.0 copy-start.2
  6.6 9.0 %all-to-all-start = ((bf16[8,1024,128]{2,1,0:T(8,128)(2,1)}), bf16[8,1024,128]{2,1,0:T(8,128)(2,1)S(1)}, u32[]{:S(2)}, u32[]{:S(2)}) async-start(bf16[8,1024,128]{2,1,0:T(8,128)(2,1)} %bitcast.22), calls=%async_computation | async-start | bytes 4194304 | tf_op jit(solution)/shard_map/all_to_all | solution.py:43
  15.7 0.0 copy-done.1
  15.7 0.0 copy-done.2
  15.7 13.0 %all_gather.6.both_ref = bf16[256,768]{1,0:T(8,128)(2,1)S(1)} all-gather(bf16[32,768]{1,0:T(8,128)(2,1)S(1)} %pad_maximum_fusion), channel_id=1, replica_groups=mesh['y'=4,'z8'=8,'zp'=2,'x'=4,'core'=2] {'x','core'}, dimensions={0}, use_global_device_ids=true | all-gather | bytes 442368 | tf_op jit(solution)/shard_map/all_gather | solution.py:210
  28.7 8.5 %all-to-all-done = bf16[8,1024,128]{2,1,0:T(8,128)(2,1)S(1)} async-done(((bf16[8,1024,128]{2,1,0:T(8,128)(2,1)}), bf16[8,1024,128]{2,1,0:T(8,128)(2,1)S(1)}, u32[]{:S(2)}, u32[]{:S(2)}) %all-to-all-start) | async-done | bytes 2097184 | tf_op jit(solution)/shard_map/all_to_all | solution.py:43
  37.2 0.3 sum_near.1
  37.4 29.3 %all_to_all.25 = bf16[8,128,128]{2,1,0:T(8,128)(2,1)S(1)} all-to-all(bf16[8,128,128]{2,1,0:T(8,128)(2,1)S(1)} %bitcast.18), channel_id=1, replica_groups={{0,64,32,96,16,80,48,112},{113,49,81,17,97,33,65,1},{2,66,34,98,18,82,5..., dimensions={0} | all-to-all | bytes 524288 | tf_op jit(solution)/shard_map/all_to_all | solution.py:43
  66.8 10.0 %all_to_all.26 = bf16[4,128,128]{2,1,0:T(8,128)(2,1)S(1)} all-to-all(bf16[4,128,128]{2,1,0:T(8,128)(2,1)S(1)} %bitcast.20), channel_id=1, replica_groups={{0,4,2,6},{1,5,3,7},{8,12,10,14},{9,13,11,15},{16,20,18,22},{17,21,19,2..., dimensions={0} | all-to-all | bytes 262144 | tf_op jit(solution)/shard_map/all_to_all | solution.py:43
  76.8 2.0 %all_gather.7.got_ref = bf16[2,4,4,32,128]{4,3,2,1,0:T(8,128)(2,1)S(1)} all-gather(bf16[1,4,4,32,128]{4,3,2,1,0:T(8,128)(2,1)S(1)} %bitcast.23), channel_id=1, replica_groups=mesh['y'=4,'z8'=8,'zp'=2,'x'=4,'core'=2] {'core'}, dimensions={0}, use_global_device_ids=true | all-gather | bytes 393216 | tf_op jit(solution)/shard_map/all_gather | solution.py:217
  78.8 1.0 middle.1
  79.8 31.9 %all_to_all.27 = bf16[8,192,128]{2,1,0:T(8,128)(2,1)S(1)} all-to-all(bf16[8,192,128]{2,1,0:T(8,128)(2,1)S(1)} %bitcast.21), channel_id=1, replica_groups={{0,64,32,96,16,80,48,112},{113,49,81,17,97,33,65,1},{2,66,34,98,18,82,5..., dimensions={0} | all-to-all | bytes 786432 | tf_op jit(solution)/shard_map/all_to_all | solution.py:43
  111.7 0.3 spread.1
  112.0 0.0 copy-start
  112.0 32.0 %all_to_all.28 = bf16[8,1088,128]{2,1,0:T(8,128)(2,1)S(1)} all-to-all(bf16[8,1088,128]{2,1,0:T(8,128)(2,1)S(1)} %bitcast.15), channel_id=1, replica_groups={{0,128,256,384,8,136,264,392},{9,137,265,393,1,129,257,385},{2,130,258,..., dimensions={0} | all-to-all | bytes 4456448 | tf_op jit(solution)/shard_map/all_to_all | solution.py:43
  144.1 0.0 copy-done
  144.1 2.6 %gather_products.1 = (bf16[32,512]{1,0:T(8,128)(2,1)}, f32[32,256]{1,0:T(8,128)}) custom-call(s32[1]{0:T(128)} %bitcast.rep_ref, s32[128]{0:T(128)} %bitcast.26, s32[128]{0:T(128)} %block_ref.3, s32[128]{0:T(128)} %src_ref.3, bf16[272,32,128]{2,1,0:T(8,128)(2,1)S(1)} %bitcast.14, bf16[128,128,128]{2,1,0:T(8,128)(2,1)S(1)} %copy-done), custom_call_target="tpu_custom_call" | custom-call | flops 134217728 | bytes 4194304 | tf_op jit(solution)/shard_map/gather_products/pallas_call | solution.py:242
  (2 shorter events, 0.0 us)
Async XLA Ops:
  6.6 9.0 %copy-start.1 = (bf16[32,512]{1,0:T(8,128)(2,1)S(1)}, bf16[32,512]{1,0:T(8,128)(2,1)}, u32[]{:S(2)}) copy-start(bf16[32,512]{1,0:T(8,128)(2,1)} %param.13) | copy-start | bytes 98308
  6.6 9.0 %copy-start.2 = (bf16[256,32]{0,1:T(8,128)(2,1)S(1)}, bf16[256,32]{0,1:T(8,128)(2,1)}, u32[]{:S(2)}) copy-start(bf16[256,32]{0,1:T(8,128)(2,1)} %param.8) | copy-start | bytes 49156
  6.6 30.5 %all-to-all-start = ((bf16[8,1024,128]{2,1,0:T(8,128)(2,1)}), bf16[8,1024,128]{2,1,0:T(8,128)(2,1)S(1)}, u32[]{:S(2)}, u32[]{:S(2)}) async-start(bf16[8,1024,128]{2,1,0:T(8,128)(2,1)} %bitcast.22), calls=%async_computation | async-start | bytes 4194304 | tf_op jit(solution)/shard_map/all_to_all | solution.py:43
  112.0 32.0 %copy-start = (bf16[128,128,128]{2,1,0:T(8,128)(2,1)S(1)}, bf16[128,128,128]{2,1,0:T(8,128)(2,1)}, u32[]{:S(2)}) copy-start(bf16[128,128,128]{2,1,0:T(8,128)(2,1)} %tiles_ref.3) | copy-start | bytes 12582916

commit v7 on v6

--- a/solution.py
+++ b/solution.py
@@ -13,7 +13,6 @@
 NY, NZ, NX, NC = 4, 16, 4, 2
 BLK = 128
 CHUNKS = (16, 48, 64)
-WRITES = 4
 NZ8, NP = NZ // 2, 2
 
 SMEM = pl.BlockSpec(memory_space=pltpu.SMEM)
@@ -28,7 +27,7 @@
 AXES = ("y", "z8", "zp", "x", "core")
 SIZES = (NY, NZ8, NP, NX, NC)
 NEAR_ORDER = [(0, 0), (1, 0), (2, 0), (3, 0), (0, 1), (1, 1), (2, 1), (3, 1)]
-FAR_ORDER = [(0,), (4,), (2,), (6,), (1,), (5,), (3,), (7,)]
+FAR_ORDER = [(0,), (2,), (4,), (6,), (1,), (3,), (5,), (7,)]
 NEAR_TURN, FAR_TURN = 4, 7
 X_ORDER = [(0,), (2,), (1,), (3,)]
 
@@ -46,7 +45,7 @@
 def slot(dest, block, core, nblk, stride):
     y, z = lax.shift_right_logical(dest, 4), dest & 15
     near = ((z & 1) * 4 + y) ^ (core * NEAR_TURN)
-    far = ((z & 2) * 2 + lax.shift_right_logical(z & 4, 1) + lax.shift_right_logical(z, 3)) ^ (core * FAR_TURN)
+    far = ((z & 2) * 2 + lax.shift_right_logical(z, 2)) ^ (core * FAR_TURN)
     return near * stride + far * nblk + block
 
 
@@ -65,7 +64,7 @@
 
 
 def scatter_products(
-    rep_ref, dest_ref, block_ref, src_ref, feats_ref, tiles_ref, out_ref, acc_ref, half_ref, buf_ref, sems, out_sems
+    rep_ref, dest_ref, block_ref, src_ref, feats_ref, tiles_ref, out_ref, acc_ref, buf_ref, sems
 ):
     copies = []
     for c, n in enumerate(CHUNKS):
@@ -85,15 +84,7 @@
                 preferred_element_type=F32,
             )
             acc_ref[slot(dest_ref[t], block_ref[t], rep_ref[0] & 1, nblk, NZ8 * nblk)] += prod
-    m = out_ref.shape[0] // WRITES
-    writes = []
-    for c in range(WRITES):
-        part = pl.ds(c * m, m)
-        half_ref[part] = acc_ref[part].astype(BF)
-        writes.append(pltpu.make_async_copy(half_ref.at[part], out_ref.at[part], out_sems.at[c]))
-        writes[c].start()
-    for c in range(WRITES):
-        writes[c].wait()
+    out_ref[...] = acc_ref[...].astype(BF)
 
 
 def gather_products(rep_ref, dest_ref, block_ref, src_ref, every_ref, tiles_ref, out_ref, wg_ref, acc_ref):
@@ -192,27 +183,23 @@
     parts = call(
         scatter_products,
         "scatter_products",
-        pltpu.HBM((ntot, panel, BLK), BF),
+        shape((ntot, panel, BLK), BF),
         [SMEM, SMEM, SMEM, SMEM, VMEM, HBM],
         [
             pltpu.VMEM((ntot, panel, BLK), F32),
-            pltpu.VMEM((ntot, panel, BLK), BF),
             pltpu.VMEM((tiles, BLK, BLK), BF),
             pltpu.SemaphoreType.DMA((len(CHUNKS),)),
-            pltpu.SemaphoreType.DMA((WRITES,)),
         ],
         flops=tile_flops,
         nbytes=tile_bytes,
-        outs=HBM,
     )(*places, in_hbm(feats), in_hbm(tile_values))
 
     got = exchange(parts.reshape(near, NZ8 * nblk, panel, BLK), ("y", "zp"), NEAR_ORDER, NEAR_TURN)
-    both = lax.all_gather(
-        jnp.concatenate([cotangent, weight.T], axis=1), ("x", "core"), axis=0, tiled=True
-    )
+    half = call(sum_first, "sum_near", shape((NZ8 * nblk, panel, BLK), BF), [VMEM], nbytes=ntot * panel * BLK * 2)(got)
+    cot, weight_t, half = lax.optimization_barrier((cotangent, weight.T, half))
+    got = exchange(half.reshape(NZ8, nblk, panel, BLK), ("z8",), FAR_ORDER, FAR_TURN)
+    both = lax.all_gather(jnp.concatenate([cot, weight_t], axis=1), ("x", "core"), axis=0, tiled=True)
     got, both = lax.optimization_barrier((got, both))
-    half = call(sum_first, "sum_near", shape((NZ8 * nblk, panel, BLK), BF), [VMEM], nbytes=ntot * panel * BLK * 2)(got)
-    got = exchange(half.reshape(NZ8, nblk, panel, BLK), ("z8",), FAR_ORDER, FAR_TURN)
     mine = call(finish_sum, "sum_far", shape((NX, nblk, panel, BLK), BF), [VMEM], nbytes=1 << 19)(got)
     gathered = lax.all_gather(exchange(mine, ("x",), X_ORDER), "core", axis=0)
 

time: 147 us -> 147 us (level)
  starting transfers between devices: 9.02 us -> 14.6 us
  waiting for transfers between devices: 8.5 us -> 3.38 us
    all_to_all x1, starting transfers between devices: 9.02 us -> 14.6 us  [exchange(): lax.all_to_all(flat, AXES, 0, 0, tiled=True, axis_index_groups=groups)]
    all_to_all x1, waiting for transfers between devices: 8.5 us -> 3.38 us  [exchange(): lax.all_to_all(flat, AXES, 0, 0, tiled=True, axis_index_groups=groups)]
where the time goes in v7:
time: 147 us; the launch traced here: 146 us
  blocking collectives  118 us (80%)
  starting transfers between devices  14.6 us (10%)
  Pallas kernels  9.68 us (7%)
  waiting for transfers between devices  3.38 us (2%)
    all_to_all x4, blocking collectives, exchange(): lax.all_to_all(flat, AXES, 0, 0, tiled=True, axis_index_groups=groups)  103 us
    all_to_all x1, starting transfers between devices, exchange(): lax.all_to_all(flat, AXES, 0, 0, tiled=True, axis_index_groups=groups)  14.6 us
    all_gather x1, blocking collectives, per_device(): lax.all_gather(jnp.concatenate([cot, weight_t], axis=1), ('x', 'core'), a...  13.3 us
    pallas_call x1, Pallas kernels, per_device(): call(scatter_products, 'scatter_products', shape((ntot, panel, BLK), BF),...  4.74 us
    all_to_all x1, waiting for transfers between devices, exchange(): lax.all_to_all(flat, AXES, 0, 0, tiled=True, axis_index_groups=groups)  3.38 us
  transfers between devices with their start and end apart: 1, of which 1 were waited for; matrix products, arithmetic and copies ran while one was open for 0% of the time, Pallas kernels for 0%

profile of v7, /device:TPU:32, one launch (start us, length us, event | category | flops | bytes accessed | tf_op | source)
XLA Modules:
  0.0 146.4 jit_solution(5677007166891003632)
XLA Ops:
  0.6 4.7 %scatter_products.1 = bf16[256,32,128]{2,1,0:T(8,128)(2,1)S(1)} custom-call(s32[1]{0:T(128)} %bitcast.rep_ref, s32[128]{0:T(128)} %bitcast.24, s32[128]{0:T(128)} %block_ref.3, s32[128]{0:T(128)} %src_ref.3, bf16[32,512]{1,0:T(8,128)(2,1)} %feats_ref.1, bf16[128,128,128]{2,1,0:T(8,128)(2,1)} %tiles_ref.3), custom_call_target="tpu_custom_call" | custom-call | flops 134217728 | bytes 4194304 | tf_op jit(solution)/shard_map/scatter_products/pallas_call | solution.py:183
  5.4 31.1 %all_to_all.25 = bf16[8,1024,128]{2,1,0:T(8,128)(2,1)S(1)} all-to-all(bf16[8,1024,128]{2,1,0:T(8,128)(2,1)S(1)} %bitcast.17), channel_id=1, replica_groups={{0,128,256,384,8,136,264,392},{9,137,265,393,1,129,257,385},{2,130,258,..., dimensions={0} | all-to-all | bytes 4194304 | tf_op jit(solution)/shard_map/all_to_all | solution.py:42
  36.5 0.0 copy-start.1
  36.5 0.0 copy-start.2
  36.5 1.0 sum_near.1
  37.5 14.6 %all-to-all-start.1 = ((bf16[8,128,128]{2,1,0:T(8,128)(2,1)}), bf16[8,128,128]{2,1,0:T(8,128)(2,1)S(1)}, u32[]{:S(2)}, u32[]{:S(2)}) async-start(bf16[8,128,128]{2,1,0:T(8,128)(2,1)} %bitcast.5), calls=%async_computation.1 | async-start | bytes 524288 | tf_op jit(solution)/shard_map/all_to_all | solution.py:42
  52.1 0.0 copy-done.1
  52.1 0.0 copy-done.2
  52.1 13.3 %all_gather.6.both_ref = bf16[256,768]{1,0:T(8,128)(2,1)S(1)} all-gather(bf16[32,768]{1,0:T(8,128)(2,1)S(1)} %pad_maximum_fusion), channel_id=1, replica_groups=mesh['y'=4,'z8'=8,'zp'=2,'x'=4,'core'=2] {'x','core'}, dimensions={0}, use_global_device_ids=true | all-gather | bytes 442368 | tf_op jit(solution)/shard_map/all_gather | solution.py:201
  65.5 3.4 %all-to-all-done.1 = bf16[8,128,128]{2,1,0:T(8,128)(2,1)S(1)} async-done(((bf16[8,128,128]{2,1,0:T(8,128)(2,1)}), bf16[8,128,128]{2,1,0:T(8,128)(2,1)S(1)}, u32[]{:S(2)}, u32[]{:S(2)}) %all-to-all-start.1) | async-done | bytes 262176 | tf_op jit(solution)/shard_map/all_to_all | solution.py:42
  68.9 9.8 %all_to_all.26 = bf16[4,128,128]{2,1,0:T(8,128)(2,1)S(1)} all-to-all(bf16[4,128,128]{2,1,0:T(8,128)(2,1)S(1)} %bitcast.20), channel_id=1, replica_groups={{0,4,2,6},{1,5,3,7},{8,12,10,14},{9,13,11,15},{16,20,18,22},{17,21,19,2..., dimensions={0} | all-to-all | bytes 262144 | tf_op jit(solution)/shard_map/all_to_all | solution.py:42
  78.7 2.0 %all_gather.7.got_ref = bf16[2,4,4,32,128]{4,3,2,1,0:T(8,128)(2,1)S(1)} all-gather(bf16[1,4,4,32,128]{4,3,2,1,0:T(8,128)(2,1)S(1)} %bitcast.22), channel_id=1, replica_groups=mesh['y'=4,'z8'=8,'zp'=2,'x'=4,'core'=2] {'core'}, dimensions={0}, use_global_device_ids=true | all-gather | bytes 393216 | tf_op jit(solution)/shard_map/all_gather | solution.py:204
  80.7 1.0 middle.1
  81.6 31.8 %all_to_all.27 = bf16[8,192,128]{2,1,0:T(8,128)(2,1)S(1)} all-to-all(bf16[8,192,128]{2,1,0:T(8,128)(2,1)S(1)} %bitcast.21), channel_id=1, replica_groups={{0,32,64,96,16,48,80,112},{113,81,49,17,97,65,33,1},{2,34,66,98,18,50,8..., dimensions={0} | all-to-all | bytes 786432 | tf_op jit(solution)/shard_map/all_to_all | solution.py:42
  113.4 0.3 spread.1
  113.8 0.0 copy-start
  113.8 30.1 %all_to_all.28 = bf16[8,1088,128]{2,1,0:T(8,128)(2,1)S(1)} all-to-all(bf16[8,1088,128]{2,1,0:T(8,128)(2,1)S(1)} %bitcast.15), channel_id=1, replica_groups={{0,128,256,384,8,136,264,392},{9,137,265,393,1,129,257,385},{2,130,258,..., dimensions={0} | all-to-all | bytes 4456448 | tf_op jit(solution)/shard_map/all_to_all | solution.py:42
  143.8 0.0 copy-done
  143.8 2.6 %gather_products.1 = (bf16[32,512]{1,0:T(8,128)(2,1)}, f32[32,256]{1,0:T(8,128)}) custom-call(s32[1]{0:T(128)} %bitcast.rep_ref, s32[128]{0:T(128)} %bitcast.25, s32[128]{0:T(128)} %block_ref.3, s32[128]{0:T(128)} %src_ref.3, bf16[272,32,128]{2,1,0:T(8,128)(2,1)S(1)} %bitcast.14, bf16[128,128,128]{2,1,0:T(8,128)(2,1)S(1)} %copy-done), custom_call_target="tpu_custom_call" | custom-call | flops 134217728 | bytes 4194304 | tf_op jit(solution)/shard_map/gather_products/pallas_call | solution.py:229
  (2 shorter events, 0.0 us)
Async XLA Ops:
  36.5 15.6 %copy-start.1 = (bf16[32,512]{1,0:T(8,128)(2,1)S(1)}, bf16[32,512]{1,0:T(8,128)(2,1)}, u32[]{:S(2)}) copy-start(bf16[32,512]{1,0:T(8,128)(2,1)} %param.13) | copy-start | bytes 98308
  36.5 15.6 %copy-start.2 = (bf16[256,32]{0,1:T(8,128)(2,1)S(1)}, bf16[256,32]{0,1:T(8,128)(2,1)}, u32[]{:S(2)}) copy-start(bf16[256,32]{0,1:T(8,128)(2,1)} %param.8) | copy-start | bytes 49156
  37.5 31.4 %all-to-all-start.1 = ((bf16[8,128,128]{2,1,0:T(8,128)(2,1)}), bf16[8,128,128]{2,1,0:T(8,128)(2,1)S(1)}, u32[]{:S(2)}, u32[]{:S(2)}) async-start(bf16[8,128,128]{2,1,0:T(8,128)(2,1)} %bitcast.5), calls=%async_computation.1 | async-start | bytes 524288 | tf_op jit(solution)/shard_map/all_to_all | solution.py:42
  113.8 30.1 %copy-start = (bf16[128,128,128]{2,1,0:T(8,128)(2,1)S(1)}, bf16[128,128,128]{2,1,0:T(8,128)(2,1)}, u32[]{:S(2)}) copy-start(bf16[128,128,128]{2,1,0:T(8,128)(2,1)} %tiles_ref.3) | copy-start | bytes 12582916
